TPU v7x, 256 devices: a whole 4x4x8 slice. The times are simulated.
256 devices in a mesh: prompt: 16 (over y, x), member: 16 (over z, core).
Axes of the slice: x: 4, y: 4, z: 8, core: 2. Of those that a mesh axis runs over, the one named last changes fastest.
Arguments:
- queries: bfloat16 [16, 2048, 4096], P('prompt', 'member'), may hold values from -6 to 6
- out_grad: bfloat16 [16, 2048, 4096], P('prompt', 'member'), may hold values from -6 to 6
- log_norms: float32 [16, 32, 2048], P('prompt', None, 'member'), may hold values from 5.5 to 7.5
- row_deltas: float32 [16, 32, 2048], P('prompt', None, 'member'), may hold values from -8 to 8
- prompt_kv: bfloat16 [16, 2, 2048, 256], P('prompt', None, 'member'), may hold values from -6 to 6
- grad_rows: bfloat16 [2048, 4096], P('prompt', 'member'), may hold values from -1.1953125 to 1.1953125
- hidden_acts: bfloat16 [2048, 8, 1536], P('prompt'), may hold values from -6 to 6
- route_weight: float32 [2048, 8], P('prompt'), may hold values from 0.02 to 0.5
- expert_ids: int32 [2048, 8], P('prompt'), may hold values from 0 to 63, all different within a row; in each aligned block of 128 rows (0 to 127, 128 to 255, ...) at most 32 rows name the same one
- w_down: bfloat16 [64, 1536, 4096], P('prompt', None, 'member'), may hold values from -0.15625 to 0.15625
Outputs:
- query_grad: bfloat16 [16, 2048, 4096], P('prompt', 'member')
- prompt_kv_grad: float32 [16, 2, 2048, 256], P('prompt', None, 'member')
- w_down_grad: bfloat16 [64, 1536, 4096], P('prompt', None, 'member')
- route_grad: float32 [2048, 8], P('prompt')
Inputs may be any that keep to these rules, and one draw needn't show every extreme that they name: `expert_ids`: within each aligned block of 128 rows (the rows of one prompt group) the 8 experts of a row differ, no expert is named by more than 32 rows of the block, a bound that some block reaches; every expert is named somewhere.
All inputs are finite; a program needn't handle non-finite values.
Results may differ from a plain program's by a relative error of at most 0.0057.
Values may be sent and summed in bfloat16 or wider, within the bound.
No kernel may reach another device: no remote copies, remote signals or barrier semaphores. Data moves between devices by JAX's collectives and lax.ppermute only.
A program may use at most 192 MiB of HBM per device.

v0:
```python
import jax
import jax.numpy as jnp
from jax import lax
from jax.sharding import PartitionSpec as P

QH = 32
KVH = 2
HD = 128
EFF = 1536
TOPK = 8
CAP = 32


def attend_piece(shard_piece, query_heads, grad_heads, norm_block, delta_block):
    scale = HD ** (-0.5)
    key_count = shard_piece.shape[2]
    key_heads = shard_piece[0, 0].reshape(key_count, KVH, HD)
    value_heads = shard_piece[0, 1].reshape(key_count, KVH, HD)
    scores = (
        jnp.einsum("rkgd,nkd->kgrn", query_heads, key_heads, preferred_element_type=jnp.float32)
        * scale
    )
    probs = jnp.exp(scores - norm_block[..., None])
    probs_low = probs.astype(jnp.bfloat16)
    value_term = jnp.einsum(
        "kgrn,rkgd->nkd", probs_low, grad_heads, preferred_element_type=jnp.float32
    )
    dprob = jnp.einsum(
        "rkgd,nkd->kgrn", grad_heads, value_heads, preferred_element_type=jnp.float32
    )
    dscore = (scale * probs * (dprob - delta_block[..., None])).astype(jnp.bfloat16)
    query_term = jnp.einsum("kgrn,nkd->rkgd", dscore, key_heads, preferred_element_type=jnp.float32)
    key_term = jnp.einsum("kgrn,rkgd->nkd", dscore, query_heads, preferred_element_type=jnp.float32)
    fresh = jnp.stack(
        [key_term.reshape(key_count, KVH * HD), value_term.reshape(key_count, KVH * HD)]
    )
    return (query_term, fresh)


def body(
    queries,
    out_grad,
    log_norms,
    row_deltas,
    prompt_kv,
    grad_rows,
    hidden_acts,
    route_weight,
    expert_ids,
    w_down,
):
    groups = lax.axis_size("prompt")
    group_size = QH // KVH
    resp_rows = queries.shape[1]
    shard_len = prompt_kv.shape[2]
    query_heads = queries[0].reshape(resp_rows, KVH, group_size, HD)
    grad_heads = out_grad[0].reshape(resp_rows, KVH, group_size, HD)
    norm_block = log_norms[0].reshape(KVH, group_size, resp_rows)
    delta_block = row_deltas[0].reshape(KVH, group_size, resp_rows)
    query_total, kv_total = attend_piece(
        lax.all_gather(prompt_kv, "member", axis=2, tiled=True),
        query_heads,
        grad_heads,
        norm_block,
        delta_block,
    )
    query_grad = query_total.reshape(1, resp_rows, QH * HD).astype(jnp.bfloat16)
    summed = lax.psum(kv_total, "member")
    own_share = lax.dynamic_slice_in_dim(summed, lax.axis_index("member") * shard_len, shard_len, 1)
    prompt_kv_grad = own_share[None]
    token_count = grad_rows.shape[0]
    width_share = grad_rows.shape[1]
    local_experts = w_down.shape[0]
    experts_all = local_experts * groups
    route_count = token_count * TOPK
    flat_ids = expert_ids.reshape(-1)
    matches = (flat_ids[:, None] == jnp.arange(experts_all, dtype=jnp.int32)[None, :]).astype(
        jnp.int32
    )
    position = jnp.sum((jnp.cumsum(matches, axis=0) - 1) * matches, axis=1)
    slot_index = flat_ids * CAP + position
    slot_total = experts_all * CAP
    spread_hidden = (
        jnp.zeros((slot_total, EFF), jnp.bfloat16)
        .at[slot_index]
        .set(hidden_acts.reshape(route_count, EFF))
    )
    spread_grad = (
        jnp.zeros((slot_total, width_share), jnp.bfloat16)
        .at[slot_index]
        .set(jnp.repeat(grad_rows, TOPK, axis=0))
    )
    spread_weight = (
        jnp.zeros((slot_total,), jnp.bfloat16)
        .at[slot_index]
        .set(route_weight.reshape(-1).astype(jnp.bfloat16))
    )
    spread_hidden = spread_hidden.reshape(groups, local_experts, CAP, EFF)
    spread_grad = spread_grad.reshape(groups, local_experts, CAP, width_share)
    spread_weight = spread_weight.reshape(groups, local_experts, CAP)
    got_hidden, got_grad, got_weight = (
        lax.all_to_all(spread_hidden, "prompt", split_axis=0, concat_axis=0, tiled=True),
        lax.all_to_all(spread_grad, "prompt", split_axis=0, concat_axis=0, tiled=True),
        lax.all_to_all(spread_weight, "prompt", split_axis=0, concat_axis=0, tiled=True),
    )
    scaled = (got_weight.astype(jnp.float32)[..., None] * got_grad.astype(jnp.float32)).astype(
        jnp.bfloat16
    )
    w_down_grad = jnp.einsum(
        "pecf,pecd->efd", got_hidden, scaled, preferred_element_type=jnp.float32
    ).astype(jnp.bfloat16)
    expert_out = jnp.einsum(
        "pecf,efd->pecd", got_hidden, w_down, preferred_element_type=jnp.float32
    )
    partial_dots = jnp.sum(expert_out * got_grad.astype(jnp.float32), axis=3)
    returned = lax.all_to_all(partial_dots, "prompt", split_axis=0, concat_axis=0, tiled=True)
    route_part = returned.reshape(-1)[slot_index].reshape(token_count, TOPK)
    route_grad = lax.psum(route_part, "member")
    return (query_grad, prompt_kv_grad, w_down_grad, route_grad)


def solution(mesh):
    return jax.shard_map(
        body,
        mesh=mesh,
        in_specs=(
            P("prompt", "member", None),
            P("prompt", "member", None),
            P("prompt", None, "member"),
            P("prompt", None, "member"),
            P("prompt", None, "member", None),
            P("prompt", "member"),
            P("prompt", None, None),
            P("prompt", None),
            P("prompt", None),
            P("prompt", None, "member"),
        ),
        out_specs=(
            P("prompt", "member", None),
            P("prompt", None, "member", None),
            P("prompt", None, "member"),
            P("prompt", None),
        ),
        check_vma=False,
    )
```

profile of v0, /device:TPU:1, one launch (start us, length us, event | category | flops | bytes accessed | tf_op | source)
XLA Modules:
  0.0 305.3 jit_solution(9790582035850929380)
XLA Ops:
  7.2 0.0 copy-start
  7.2 0.0 all-gather.2.cloned.1.call-start
  7.2 1.8 copy.141
  9.0 0.0 all-gather.2.cloned.1.call-update
  9.1 0.8 copy.153
  9.9 0.1 eq.29
  9.9 0.1 eq.25
  10.0 0.7 broadcast_multiply_fusion
  10.7 0.1 copy.152
  10.8 0.1 mul.52
  10.9 0.7 fusion.25
  11.7 31.1 %reduce-window.6 = s32[64,8,128]{2,1,0:T(8,128)S(1)} reduce-window(s32[64,8,128]{2,1,0:T(8,128)} %fusion.25, s32[]{:T(128)} %constant.10.clone.1), window={size=1x1x128 pad=0_0x0_0x127_0}, to_apply=%region_1.0 | reduce-window | flops 8323072 | bytes 524292 | tf_op jit(solution)/shard_map/reduce-window
  42.8 0.8 slice.20
  43.6 1.1 copy.155
  44.8 0.1 copy.156
  44.8 0.7 convert_element_type.53
  45.5 0.1 copy.157
  45.7 0.1 reshape.124
  45.8 0.1 add_add_fusion
  45.9 0.1 fusion.23
  46.0 7.6 %scatter_custom_fusion.1 = bf16[2048]{0:T(1024)(128)(2,1)S(1)} fusion(s32[1024]{0:T(1024)S(1)} %bitcast.110, bf16[1024]{0:T(1024)(128)(2,1)S(1)} %reshape.124, bf16[]{:T(256)} %constant.14.clone.1), kind=kCustom, calls=%fused_computation.39 | custom fusion | bytes 4098 | tf_op jit(solution)/shard_map/scatter | solution.py:96
  53.6 0.7 reshape.99
  54.3 7.5 %all-to-all-start.1 = ((bf16[16,4,32]{2,1,0:T(4,128)(2,1)}), bf16[16,4,32]{2,1,0:T(4,128)(2,1)S(1)}, u32[]{:S(2)}, u32[]{:S(2)}) async-start(bf16[16,4,32]{2,1,0:T(4,128)(2,1)} %reshape.99), calls=%async_computation.1 | async-start | bytes 32768 | tf_op jit(solution)/shard_map/all_to_all | solution.py:104
  61.9 2.3 copy.178
  64.1 2.3 copy.179
  66.4 9.1 %scatter_custom_fusion = bf16[2048,1536]{1,0:T(8,128)(2,1)} fusion(s32[1024]{0:T(1024)S(1)} %bitcast.112, bf16[128,8,1536]{2,1,0:T(8,128)(2,1)S(1)} %copy-done, bf16[]{:T(256)} %constant.14.clone.1), kind=kCustom, calls=%fused_computation.16 | custom fusion | bytes 9437186 | tf_op jit(solution)/shard_map/scatter | solution.py:86
  75.6 6.0 %scatter_custom_fusion.2 = bf16[2048,256]{1,0:T(8,128)(2,1)} fusion(s32[1024]{0:T(1024)S(1)} %bitcast.113, bf16[]{:T(256)} %constant.14.clone.1, bf16[128,256]{1,0:T(8,128)(2,1)S(1)} %copy-done.6), kind=kCustom, calls=%fused_computation.25 | custom fusion | bytes 1114114 | tf_op jit(solution)/shard_map/scatter | solution.py:91
  81.6 0.0 all-to-all-done.1
  81.6 6.7 %all-to-all-start.2 = ((bf16[16,4,32,256]{3,2,1,0:T(8,128)(2,1)}), bf16[16,4,32,256]{3,2,1,0:T(8,128)(2,1)S(1)}, u32[]{:S(2)}, u32[]{:S(2)}) async-start(bf16[16,4,32,256]{3,2,1,0:T(8,128)(2,1)} %bitcast.28), calls=%async_computation.2 | async-start | bytes 2097152 | tf_op jit(solution)/shard_map/all_to_all | solution.py:103
  88.3 0.0 all-gather.2.cloned.1.call-done
  88.3 2.8 fusion.29
  91.1 13.1 %fusion.30 = f32[2,2048,128,16]{2,1,3,0:T(8,128)} fusion(bf16[2048,2,128,1]{0,2,3,1:T(8,128)(2,1)S(1)} %bitcast.97, bf16[128,2,16,128]{0,3,2,1:T(8,128)(2,1)S(1)} %bitcast.95), kind=kOutput, calls=%fused_computation.45 | convolution fusion | flops 2147483648 | bytes 35651584 | tf_op jit(solution)/shard_map/rkgd,nkd->kgrn/dot_general | solution.py:20
  104.2 0.0 all-to-all-done.2
  104.2 1.0 copy-done.4
  105.2 6.8 %all-to-all-start = ((bf16[16,4,32,1536]{3,2,1,0:T(8,128)(2,1)}), bf16[16,4,32,1536]{3,2,1,0:T(8,128)(2,1)}, u32[]{:S(2)}, u32[]{:S(2)}) async-start(bf16[16,4,32,1536]{3,2,1,0:T(8,128)(2,1)} %bitcast.93), calls=%async_computation | async-start | bytes 12582912 | tf_op jit(solution)/shard_map/all_to_all | solution.py:102
  112.0 0.0 all-reduce.2.cloned.1.call-start
  112.1 0.0 copy-done.3
  112.1 0.0 copy-done.7
  112.1 0.0 copy-done.8
  112.1 20.4 %fusion.1 = bf16[2,16,128,2048]{2,3,1,0:T(8,128)(2,1)} fusion(f32[2,2048,128,16]{2,1,3,0:T(8,128)} %fusion.30, f32[2,16,128]{2,1,0:T(8,128)S(1)} %bitcast.114, f32[2,16,128]{2,1,0:T(8,128)S(1)} %bitcast.106, bf16[2048,2,128,1]{0,2,3,1:T(8,128)(2,1)} %bitcast.104, bf16[128,2,16,128]{0,3,2,1:T(8,128)(2,1)S(1)} %bitcast.102), kind=kOutput, calls=%fused_computation.6 | convolution fusion | flops 2197815296 | bytes 52461568 | tf_op jit(solution)/shard_map/rkgd,nkd->kgrn/dot_general | solution.py:28
  132.5 8.1 %convolution_convert_fusion = bf16[2,16,128,128]{2,3,1,0:T(8,128)(2,1)S(1)} fusion(bf16[2048,2,128,1]{0,2,3,1:T(8,128)(2,1)S(1)} %bitcast.98, bf16[2,16,128,2048]{2,3,1,0:T(8,128)(2,1)} %fusion.1), kind=kOutput, calls=%fused_computation.23 | convolution fusion | flops 2148007936 | bytes 18874368 | tf_op jit(solution)/shard_map/kgrn,nkd->rkgd/dot_general | solution.py:32
  140.7 1.3 copy.163
  142.0 9.0 %fusion.31 = f32[2,2048,128,1]{1,2,3,0:T(8,128)S(1)} fusion(bf16[2,16,128,2048]{2,3,1,0:T(8,128)(2,1)} %fusion.1, bf16[128,2,16,128]{0,3,2,1:T(8,128)(2,1)S(1)} %bitcast.96), kind=kOutput, calls=%fused_computation.46 | convolution fusion | flops 2147483648 | bytes 19922944 | tf_op jit(solution)/shard_map/kgrn,rkgd->nkd/dot_general | solution.py:33
  151.0 15.4 %fusion.4 = f32[2,2048,128,1]{1,2,3,0:T(8,128)} fusion(bf16[128,2,16,128]{0,3,2,1:T(8,128)(2,1)} %bitcast.101, f32[2,2048,128,16]{2,1,3,0:T(8,128)} %fusion.30, f32[2,16,128]{2,1,0:T(8,128)S(1)} %bitcast.107), kind=kOutput, calls=%fused_computation.10 | convolution fusion | flops 2172649472 | bytes 36716544 | tf_op jit(solution)/shard_map/kgrn,rkgd->nkd/dot_general | solution.py:25
  166.4 4.1 %pad_maximum_fusion = f32[2,2048,256]{1,2,0:T(8,128)} fusion(f32[1,2048,256]{1,2,0:T(8,128)} %bitcast.99, f32[1,2048,256]{1,2,0:T(8,128)S(1)} %bitcast.94), kind=kLoop, calls=%fused_computation.14 | loop fusion | flops 1048576 | bytes 8388608 | tf_op jit(solution)/shard_map/stack | solution.py:34
  170.6 0.0 all-reduce.2.cloned.1.call-update
  170.6 31.8 %all-to-all-done = bf16[16,4,32,1536]{3,2,1,0:T(8,128)(2,1)} async-done(((bf16[16,4,32,1536]{3,2,1,0:T(8,128)(2,1)}), bf16[16,4,32,1536]{3,2,1,0:T(8,128)(2,1)}, u32[]{:S(2)}, u32[]{:S(2)}) %all-to-all-start) | async-done | bytes 6291488 | tf_op jit(solution)/shard_map/all_to_all | solution.py:102
  202.4 5.6 %fusion.13 = f32[16,4,32]{2,0,1:T(8,128)S(1)} fusion(bf16[4,1536,256]{2,1,0:T(8,128)(2,1)} %param.19, bf16[16,4,32,1536]{3,2,1,0:T(8,128)(2,1)} %all-to-all-done, bf16[16,4,32,256]{3,2,1,0:T(8,128)(2,1)S(1)} %copy-done.5), kind=kOutput, calls=%fused_computation.22 | convolution fusion | flops 1612183552 | bytes 10493952 | tf_op jit(solution)/shard_map/pecf,efd->pecd/dot_general | solution.py:112
  208.1 0.7 reshape.149
  208.7 4.7 %all-to-all-start.3 = ((f32[16,1,128]{2,1,0:T(1,128)}), f32[16,1,128]{2,1,0:T(1,128)S(1)}, u32[]{:S(2)}, u32[]{:S(2)}) async-start(f32[16,1,128]{2,1,0:T(1,128)} %reshape.149), calls=%async_computation.3 | async-start | bytes 16384 | tf_op jit(solution)/shard_map/all_to_all | solution.py:116
  213.4 0.0 copy-start.1
  213.4 7.5 %bitcast_convert_fusion = bf16[4,1536,256]{2,1,0:T(8,128)(2,1)} fusion(bf16[16,4,32,1536]{3,2,1,0:T(8,128)(2,1)} %all-to-all-done, f32[16,4,32]{2,0,1:T(8,128)S(1)} %copy_convert_fusion, bf16[16,4,32,256]{3,2,1,0:T(8,128)(2,1)} %copy-done.4), kind=kOutput, calls=%fused_computation.11 | convolution fusion | flops 1613758464 | bytes 10493952 | tf_op jit(solution)/shard_map/pecf,pecd->efd/dot_general | solution.py:109
  220.9 0.0 all-to-all-done.3
  220.9 0.5 broadcast.78
  221.4 0.7 reduce
  222.1 0.1 reshape.150
  222.2 0.1 reshape.102
  222.3 6.1 %gather_fusion = f32[1024]{0:T(1024)S(1)} fusion(f32[2048]{0:T(1024)S(1)} %reshape.102, s32[1024]{0:T(1024)S(1)} %broadcast_clamp_fusion), kind=kCustom, calls=%fused_computation | custom fusion | bytes 12288 | tf_op jit(solution)/shard_map/gather | solution.py:117
  228.4 0.1 reshape.103
  228.5 48.5 %psum.15 = f32[128,8]{1,0:T(8,128)S(1)} all-reduce(f32[128,8]{1,0:T(8,128)S(1)} %reshape.103), channel_id=1, replica_groups=mesh['prompt'=16,'member'=16] {'member'}, use_global_device_ids=true, to_apply=%region_8.9 | all-reduce | flops 1024 | bytes 8192 | tf_op jit(solution)/shard_map/psum | solution.py:118
  277.0 0.7 copy.164
  277.7 18.9 %all-reduce.2.cloned.1.call-done = f32[2,2048,256]{1,2,0:T(8,128)} async-done(((f32[2,2048,256]{1,2,0:T(8,128)}), f32[2,2048,256]{1,2,0:T(8,128)}) %all-reduce.2.cloned.1.call-update) | async-done | bytes 4194320 | tf_op jit(solution)/shard_map/psum | solution.py:68
  296.6 1.0 constant_dynamic-slice_fusion
  297.6 0.8 copy.151
  (18 shorter events, 0.1 us)
Async XLA Ops:
  7.2 59.3 %copy-start = (bf16[128,8,1536]{2,1,0:T(8,128)(2,1)S(1)}, bf16[128,8,1536]{2,1,0:T(8,128)(2,1)}, u32[]{:S(2)}) copy-start(bf16[128,8,1536]{2,1,0:T(8,128)(2,1)} %param.16) | copy-start | bytes 9437188
  7.2 81.1 %all-gather.2.cloned.1.call-start = ((), (), s32[]{:S(2)}) async-start(), calls=%async_computation.4 | async-start | bytes 2228224 | tf_op jit(solution)/shard_map/all_gather | solution.py:61
  54.3 27.3 %all-to-all-start.1 = ((bf16[16,4,32]{2,1,0:T(4,128)(2,1)}), bf16[16,4,32]{2,1,0:T(4,128)(2,1)S(1)}, u32[]{:S(2)}, u32[]{:S(2)}) async-start(bf16[16,4,32]{2,1,0:T(4,128)(2,1)} %reshape.99), calls=%async_computation.1 | async-start | bytes 32768 | tf_op jit(solution)/shard_map/all_to_all | solution.py:104
  64.1 11.5 %copy-start.6 = (bf16[128,256]{1,0:T(8,128)(2,1)S(1)}, bf16[128,256]{1,0:T(8,128)(2,1)}, u32[]{:S(2)}) copy-start(bf16[128,256]{1,0:T(8,128)(2,1)} %param.15) | copy-start | bytes 196612
  75.6 15.5 %copy-start.2 = (bf16[1,128,4096]{1,2,0:T(8,128)(2,1)S(1)}, bf16[1,128,4096]{1,2,0:T(8,128)(2,1)}, u32[]{:S(2)}) copy-start(bf16[1,128,4096]{1,2,0:T(8,128)(2,1)} %copy.178) | copy-start | bytes 3145732
  81.6 22.6 %all-to-all-start.2 = ((bf16[16,4,32,256]{3,2,1,0:T(8,128)(2,1)}), bf16[16,4,32,256]{3,2,1,0:T(8,128)(2,1)S(1)}, u32[]{:S(2)}, u32[]{:S(2)}) async-start(bf16[16,4,32,256]{3,2,1,0:T(8,128)(2,1)} %bitcast.28), calls=%async_computation.2 | async-start | bytes 2097152 | tf_op jit(solution)/shard_map/all_to_all | solution.py:103
  104.2 1.0 copy-start.4
  105.2 6.9 %copy-start.3 = (bf16[1,128,4096]{1,2,0:T(8,128)(2,1)S(1)}, bf16[1,128,4096]{1,2,0:T(8,128)(2,1)}, u32[]{:S(2)}) copy-start(bf16[1,128,4096]{1,2,0:T(8,128)(2,1)} %copy.179) | copy-start | bytes 3145732
  105.2 6.9 %copy-start.7 = (f32[1,32,128]{2,1,0:T(8,128)S(1)}, f32[1,32,128]{2,1,0:T(8,128)}, u32[]{:S(2)}) copy-start(f32[1,32,128]{2,1,0:T(8,128)} %param.12) | copy-start | bytes 49156
  105.2 6.9 %copy-start.8 = (f32[1,32,128]{2,1,0:T(8,128)S(1)}, f32[1,32,128]{2,1,0:T(8,128)}, u32[]{:S(2)}) copy-start(f32[1,32,128]{2,1,0:T(8,128)} %param.13) | copy-start | bytes 49156
  105.2 97.2 %all-to-all-start = ((bf16[16,4,32,1536]{3,2,1,0:T(8,128)(2,1)}), bf16[16,4,32,1536]{3,2,1,0:T(8,128)(2,1)}, u32[]{:S(2)}, u32[]{:S(2)}) async-start(bf16[16,4,32,1536]{3,2,1,0:T(8,128)(2,1)} %bitcast.93), calls=%async_computation | async-start | bytes 12582912 | tf_op jit(solution)/shard_map/all_to_all | solution.py:102
  112.0 184.6 %all-reduce.2.cloned.1.call-start = ((), (), s32[]{:S(2)}) async-start(), calls=%async_computation.5 | async-start | bytes 8388608 | tf_op jit(solution)/shard_map/psum | solution.py:68
  166.4 36.0 %copy-start.5 = (bf16[16,4,32,256]{3,2,1,0:T(8,128)(2,1)S(1)}, bf16[16,4,32,256]{3,2,1,0:T(8,128)(2,1)}, u32[]{:S(2)}) copy-start(bf16[16,4,32,256]{3,2,1,0:T(8,128)(2,1)} %copy-done.4) | copy-start | bytes 3145732
  208.7 12.2 %all-to-all-start.3 = ((f32[16,1,128]{2,1,0:T(1,128)}), f32[16,1,128]{2,1,0:T(1,128)S(1)}, u32[]{:S(2)}, u32[]{:S(2)}) async-start(f32[16,1,128]{2,1,0:T(1,128)} %reshape.149), calls=%async_computation.3 | async-start | bytes 16384 | tf_op jit(solution)/shard_map/all_to_all | solution.py:116
  213.4 85.0 %copy-start.1 = (bf16[128,8,1536]{2,1,0:T(8,128)(2,1)S(1)}, bf16[128,8,1536]{2,1,0:T(8,128)(2,1)}, u32[]{:S(2)}) copy-start(bf16[128,8,1536]{2,1,0:T(8,128)(2,1)} %param.16) | copy-start | bytes 9437188
Sparse Core Ops, SparseCore 0:
  10.3 45.1 all-gather.1
  170.7 125.8 all-reduce.1
where the time goes:
time: 307 us; the launch traced here: 305 us
  matrix products  79.2 us (26%)
  waiting for transfers between devices  50.8 us (17%)
  local copies, waits for them, and re-layouts  48.5 us (16%)
  blocking collectives  48.5 us (16%)
  other arithmetic  38.3 us (12%)
  starting transfers between devices  25.8 us (8%)
  between operations  14.3 us (5%)
    psum x1, blocking collectives, body(): route_grad = lax.psum(route_part, 'member')  48.5 us
    all_to_all x1, waiting for transfers between devices, body(): lax.all_to_all(spread_hidden, 'prompt', split_axis=0, concat_axis=0, tile...  31.8 us
    another operation x2, other arithmetic  31.1 us
    dot_general x1, matrix products, attend_piece(): jnp.einsum('rkgd,nkd->kgrn', grad_heads, value_heads, preferred_element_t...  20.4 us
    psum x1, waiting for transfers between devices, body(): summed = lax.psum(kv_total, 'member')  18.9 us
    dot_general x1, matrix products, attend_piece(): jnp.einsum('kgrn,rkgd->nkd', probs_low, grad_heads, preferred_element_typ...  15.4 us
    dot_general x1, matrix products, attend_piece(): jnp.einsum('rkgd,nkd->kgrn', query_heads, key_heads, preferred_element_ty...  13.1 us
    scatter x1, local copies, waits for them, and re-layouts, body(): spread_hidden = jnp.zeros((slot_total, EFF), jnp.bfloat16).at[slot_index]...  9.15 us
  transfers between devices with their start and end apart: 6, of which 2 were waited for; matrix products, arithmetic and copies ran while one was open for 53% of the time, Pallas kernels for 0%

commit v1 on v0

v1 whole, which is shorter than its diff:
```python
import functools
import math

import jax
import jax.numpy as jnp
from jax import lax
from jax.experimental import pallas as pl
from jax.experimental.pallas import tpu as pltpu
from jax.sharding import Mesh, PartitionSpec as P

QH = 32
KVH = 2
HD = 128
GROUP = QH // KVH
EFF = 1536
HALF = EFF // 2
TOPK = 8
CAP = 32
TOK = 128
ROUTES = TOK * TOPK
LOCAL = 4
EXPERTS = 64
SLOTS = LOCAL * CAP
DSTS = 4
NP = 16
NZ = 8
WID = 256
SCALE = HD ** (-0.5)
LOG2E = math.log2(math.e)
BF = jnp.bfloat16
F32 = jnp.float32
VMEM = 60 << 20
HEADS = 4
SWAP = [(0, 1), (1, 0)]


def shift(n, by):
    return [(i, (i + by) % n) for i in range(n)]


def cost(flops, moved, exps=0):
    return pl.CostEstimate(flops=flops, bytes_accessed=moved, transcendentals=exps)


def dot(a, b, ca=1, cb=0):
    return lax.dot_general(a, b, (((ca,), (cb,)), ((), ())), preferred_element_type=F32)


def iota(shape, dim):
    return lax.broadcasted_iota(jnp.int32, shape, dim)


def upper(n):
    return (iota((n, n), 0) < iota((n, n), 1)).astype(BF)


def dispatch_kernel(
    c_ref, ids_ref, w_ref, grad_ref, hid_ref, down_ref, out_ref, slot_ref, give_ref, row_ref
):
    give_ref[...] = down_ref[...]

    @pl.when(pl.program_id(0) == 0)
    def _():
        ids = ids_ref[...]
        hots = [(ids[k : k + 1] == iota((EXPERTS, TOK), 0)).astype(F32) for k in range(TOPK)]
        before = dot(sum(hots).astype(BF), upper(TOK))
        place = jnp.concatenate(
            [jnp.sum(h * before, axis=0, keepdims=True) for h in hots], axis=0
        )
        slot_ref[...] = ids * CAP + place.astype(jnp.int32)
        token = (iota((TOK, ROUTES), 0) == iota((TOK, ROUTES), 1) // TOPK).astype(F32).astype(BF)
        choice = (iota((TOPK, ROUTES), 0) == iota((TOPK, ROUTES), 1) % TOPK).astype(F32)
        wide = dot(ids.astype(F32).astype(BF), token) * CAP + dot(place.astype(BF), token)
        row_ref[...] = jnp.sum(wide * choice, axis=0, keepdims=True).astype(jnp.int32)

    slot = slot_ref[...]
    row = row_ref[...]
    weight = w_ref[...].astype(BF).astype(F32)
    for b in range(DSTS // 2):
        first = (pl.program_id(0) * DSTS + 2 * b) * SLOTS
        pick = (row == iota((2 * SLOTS, ROUTES), 0) + first).astype(F32).astype(BF)
        rows = dot(pick, hid_ref[...]).astype(BF)
        out_ref[2 * b : 2 * b + 2, :, :HALF] = rows.reshape(2, SLOTS, HALF)
        mine = iota((2 * SLOTS, TOK), 0) + first
        scale = jnp.zeros((2 * SLOTS, TOK), F32)
        for k in range(TOPK):
            scale = jnp.where(slot[k : k + 1] == mine, weight[k : k + 1], scale)
        scaled = dot(scale.astype(BF), grad_ref[...]).astype(BF)
        out_ref[2 * b : 2 * b + 2, :, HALF:] = scaled.reshape(2, SLOTS, WID)


def dispatch(core, ids_cols, weight_cols, grad_rows, hidden, w_down):
    small = pl.BlockSpec((TOPK, TOK), lambda j, c: (0, 0))
    return pl.pallas_call(
        dispatch_kernel,
        out_shape=(
            jax.ShapeDtypeStruct((NP, SLOTS, HALF + WID), BF),
            jax.ShapeDtypeStruct((TOPK, TOK), jnp.int32),
            jax.ShapeDtypeStruct((LOCAL, HALF, WID), BF),
        ),
        grid_spec=pltpu.PrefetchScalarGridSpec(
            num_scalar_prefetch=1,
            grid=(NP // DSTS,),
            in_specs=[
                small,
                small,
                pl.BlockSpec((TOK, WID), lambda j, c: (0, 0)),
                pl.BlockSpec((ROUTES, HALF), lambda j, c: (0, c[0])),
                pl.BlockSpec((1, HALF, WID), lambda j, c: (j, 1 - c[0], 0)),
            ],
            out_specs=(
                pl.BlockSpec((DSTS, SLOTS, HALF + WID), lambda j, c: (j, 0, 0)),
                small,
                pl.BlockSpec((1, HALF, WID), lambda j, c: (j, 0, 0)),
            ),
            scratch_shapes=[pltpu.VMEM((1, ROUTES), jnp.int32)],
        ),
        compiler_params=pltpu.CompilerParams(vmem_limit_bytes=VMEM),
        cost_estimate=cost(2 * NP * SLOTS * ROUTES * HALF, 6 << 20),
        name="dispatch",
    )(core, ids_cols, weight_cols, grad_rows, hidden, w_down)


def expert_kernel(c_ref, got_ref, ssib_ref, wown_ref, wsib_ref, dots_ref, own_ref, sib_ref):
    hid = got_ref[:, :, :HALF].reshape(NP * CAP, HALF)
    total = jnp.zeros((NP * CAP, HD), F32)
    for scl, w, out in (
        (got_ref[:, :, HALF:], wown_ref[0], own_ref),
        (ssib_ref[...], wsib_ref[0], sib_ref),
    ):
        scl = scl.reshape(NP * CAP, WID)
        prod = dot(hid, w) * scl.astype(F32)
        total = total + prod[:, :HD] + prod[:, HD:]
        out[0] = dot(hid, scl, 0, 0).astype(BF)
    dots_ref[0] = jnp.sum(total.T, axis=0, keepdims=True)


def experts(core, got, scl_sib, w_down, w_sib):
    half = pl.BlockSpec((1, HALF, WID), lambda e, c: (e, c[0], 0))
    return pl.pallas_call(
        expert_kernel,
        out_shape=(
            jax.ShapeDtypeStruct((LOCAL, 1, NP * CAP), F32),
            jax.ShapeDtypeStruct((LOCAL, EFF, WID), BF),
            jax.ShapeDtypeStruct((LOCAL, HALF, WID), BF),
        ),
        grid_spec=pltpu.PrefetchScalarGridSpec(
            num_scalar_prefetch=1,
            grid=(LOCAL,),
            in_specs=[
                pl.BlockSpec((NP, CAP, HALF + WID), lambda e, c: (0, e, 0)),
                pl.BlockSpec((NP, CAP, WID), lambda e, c: (0, e, 0)),
                half,
                pl.BlockSpec((1, HALF, WID), lambda e, c: (e, 0, 0)),
            ],
            out_specs=(
                pl.BlockSpec((1, 1, NP * CAP), lambda e, c: (e, 0, 0)),
                half,
                pl.BlockSpec((1, HALF, WID), lambda e, c: (e, 0, 0)),
            ),
        ),
        compiler_params=pltpu.CompilerParams(vmem_limit_bytes=VMEM),
        cost_estimate=cost(4 * LOCAL * 512 * HALF * 512, 13 << 20),
        name="experts",
    )(core, got, scl_sib, w_down, w_sib)


def join_kernel(c_ref, whole_ref, part_ref, out_ref):
    out_ref[...] = part_ref[...]


def join(core, whole, part, grid, block, whole_at, part_at, name):
    return pl.pallas_call(
        join_kernel,
        out_shape=jax.ShapeDtypeStruct(whole.shape, whole.dtype),
        grid_spec=pltpu.PrefetchScalarGridSpec(
            num_scalar_prefetch=1,
            grid=grid,
            in_specs=[pl.BlockSpec(memory_space=pl.ANY), pl.BlockSpec(block, part_at)],
            out_specs=pl.BlockSpec(block, whole_at),
        ),
        input_output_aliases={1: 0},
        compiler_params=pltpu.CompilerParams(vmem_limit_bytes=8 << 20),
        cost_estimate=cost(0, 2 * part.size * 2),
        name=name,
    )(core, whole, part)


def attend_kernel(first, last, *refs):
    c_ref, q_own, q_sib, g_own, g_sib, n_own, n_sib, d_own, d_sib, chunks = refs[:10]
    refs = refs[10:]
    if not first:
        dq_in, refs = refs[0], refs[1:]
    if last:
        dkv_out, dq_own, dq_sib, acc = refs
    else:
        dkv_out, dq_out, acc = refs
    step = pl.program_id(0)

    @pl.when(step == 0)
    def _():
        acc[...] = jnp.zeros_like(acc)

    heads = range(HEADS)
    cols = [slice(i * HD, (i + 1) * HD) for i in heads]
    q = jnp.concatenate([r[0, :, s] for s in cols for r in (q_own, q_sib)], axis=0)
    g = jnp.concatenate([r[0, :, s] for s in cols for r in (g_own, g_sib)], axis=0)

    def rows(own, sib):
        parts = []
        for i in heads:
            h = c_ref[0] * GROUP + step * HEADS + i
            parts += [own[0, pl.ds(h, 1), :], sib[0, pl.ds(h, 1), :]]
        return jnp.concatenate(parts, axis=1)

    norm = rows(n_own, n_sib) * LOG2E - math.log2(SCALE)
    delta = rows(d_own, d_sib)
    total = None
    for i in range(chunks.shape[0]):
        k, v = chunks[i, 0], chunks[i, 1]
        probs = jnp.exp2(dot(k, q, 1, 1) * (SCALE * LOG2E) - norm)
        dscore = (probs * (dot(v, g, 1, 1) - delta)).astype(BF)
        acc[i, 0] += dot(dscore, q)
        acc[i, 1] += dot(probs.astype(BF), g)
        term = dot(k, dscore, 0, 0)
        total = term if total is None else total + term
    total = total.T
    for i in heads:
        piece = total[i * 2 * HD : (i + 1) * 2 * HD]
        if not first:
            piece = piece + dq_in[:, cols[i]]
        if last:
            dq_own[0, :, cols[i]] = piece[:HD].astype(BF)
            dq_sib[:, cols[i]] = piece[HD:].astype(BF)
        else:
            dq_out[:, cols[i]] = piece

    @pl.when(step == GROUP // HEADS - 1)
    def _():
        dkv_out[:, 0] = acc[:, 0].astype(dkv_out.dtype)
        dkv_out[:, 1] = (acc[:, 1] * (1.0 / SCALE)).astype(dkv_out.dtype)


def attend(core, rows, chunks, kind, dq=None, last=False):
    first = dq is None
    count = chunks.shape[0]
    span = HEADS * HD
    wide = pl.BlockSpec((1, HD, span), lambda h, c: (0, 0, c[0] * (GROUP // HEADS) + h))
    line = pl.BlockSpec((1, QH, HD), lambda h, c: (0, 0, 0))
    keys = pl.BlockSpec(chunks.shape, lambda h, c: (0, 0, 0, 0))
    both = pl.BlockSpec((2 * HD, span), lambda h, c: (0, h))
    one = pl.BlockSpec((HD, span), lambda h, c: (0, h))
    in_specs = [wide] * 4 + [line] * 4 + [keys]
    args = [arr for pair in rows for arr in pair] + [chunks]
    outs = [jax.ShapeDtypeStruct(chunks.shape, kind)]
    out_specs = [keys]
    if not first:
        in_specs.append(both)
        args.append(dq)
    if last:
        outs += [
            jax.ShapeDtypeStruct((1, HD, QH * HD), BF),
            jax.ShapeDtypeStruct((HD, GROUP * HD), BF),
        ]
        out_specs += [wide, one]
    else:
        outs += [jax.ShapeDtypeStruct((2 * HD, GROUP * HD), F32)]
        out_specs += [both]
    return pl.pallas_call(
        functools.partial(attend_kernel, first, last),
        out_shape=tuple(outs),
        grid_spec=pltpu.PrefetchScalarGridSpec(
            num_scalar_prefetch=1,
            grid=(GROUP // HEADS,),
            in_specs=in_specs,
            out_specs=tuple(out_specs),
            scratch_shapes=[pltpu.VMEM(chunks.shape, F32)],
        ),
        compiler_params=pltpu.CompilerParams(vmem_limit_bytes=VMEM),
        cost_estimate=cost(
            10 * count * GROUP * 256 * 256 * 256, 8 << 20, count * GROUP * 256 * 256
        ),
        name=f"attend_{count}",
    )(core, *args)


def collect_kernel(slot_ref, w_ref, got_ref, out_ref):
    turned = jnp.sum(got_ref[...].reshape(NP, NZ, SLOTS), axis=1).T
    for k in range(TOPK):
        slot = slot_ref[k : k + 1, :]
        total = jnp.zeros((8, TOK), F32)
        for p in range(NP):
            want = iota((SLOTS, TOK), 0) + p * SLOTS
            hit = jnp.where(slot == want, turned[:, p : p + 1], 0.0)
            total = total + jnp.sum(hit.reshape(SLOTS // 8, 8, TOK), axis=0)
        out_ref[k : k + 1, :] = jnp.sum(total, axis=0, keepdims=True)
    out_ref[...] = out_ref[...] / w_ref[...].astype(BF).astype(F32)


def collect(slot, weight_cols, got):
    return pl.pallas_call(
        collect_kernel,
        out_shape=jax.ShapeDtypeStruct((TOPK, TOK), F32),
        compiler_params=pltpu.CompilerParams(vmem_limit_bytes=VMEM),
        cost_estimate=cost(8 << 20, 1 << 18),
        name="collect",
    )(slot, weight_cols, got)


def body(
    queries,
    out_grad,
    log_norms,
    row_deltas,
    prompt_kv,
    grad_rows,
    hidden_acts,
    route_weight,
    expert_ids,
    w_down,
):
    c = lax.axis_index("c")
    core = c.astype(jnp.int32)[None]
    prompt = lax.axis_index("prompt").astype(jnp.int32)[None]

    def swap(x):
        return lax.ppermute(x, "c", SWAP)

    def across(x, by):
        return lax.ppermute(x, "z", [(i, i ^ by) for i in range(NZ)])

    own = jnp.concatenate([prompt_kv[0], swap(prompt_kv[0])], axis=1)
    own = jnp.where(c == 0, own[:, :, :HD], own[:, :, HD:])[None]

    ids_cols, weight_cols = expert_ids.T, route_weight.T
    sent, slot, w_give = dispatch(
        core, ids_cols, weight_cols, grad_rows, hidden_acts.reshape(ROUTES, EFF), w_down
    )
    sibs = [swap(x) for x in (queries, out_grad, log_norms, row_deltas)]
    sent, sibs, own = lax.optimization_barrier((sent, sibs, own))
    rows = list(zip((queries, out_grad, log_norms, row_deltas), sibs))
    got = lax.all_to_all(sent, "prompt", 0, 0, tiled=True)
    keys = [own] + [across(own, k) for k in (4, 2, 6)]
    keys_a = jnp.concatenate(keys[:2], axis=0)
    keys_c = jnp.concatenate(keys[2:], axis=0)
    keys_b = across(jnp.concatenate([keys_a, keys_c], axis=0), 1)
    w_sib = swap(w_give)

    kv_a, dq = attend(core, rows, keys_a, F32)
    kv_b, dq = attend(core, rows, keys_b, BF, dq)
    kv_c, query_grad, query_sib = attend(core, rows, keys_c, F32, dq, last=True)
    kv_b = across(kv_b, 1)
    kv_a, kv_b, kv_c = lax.optimization_barrier((kv_a, kv_b, kv_c))
    kv_b = kv_b.astype(F32)
    kv_a, kv_c = kv_a + kv_b[:2], (kv_c + kv_b[2:]).astype(BF)
    kv_parts = [
        across(kv_a[1].astype(BF), 4),
        across(kv_c[0], 2),
        across(kv_c[1], 6),
    ]
    got, kv_parts, query_sib = lax.optimization_barrier((got, kv_parts, query_sib))
    query_sib = swap(query_sib[None])

    dots, w_down_grad, w_part = experts(core, got, swap(got[:, :, HALF:]), w_down, w_sib)
    dots = dots + swap(dots)
    dots = jnp.transpose(dots.reshape(LOCAL, NP, CAP), (1, 0, 2)).reshape(NP, 1, SLOTS)
    dots = jnp.broadcast_to(dots, (NP, NZ, SLOTS)).reshape(NP * NZ, SLOTS)
    kv_sum = kv_a[0]
    for part in kv_parts:
        kv_sum = kv_sum + part.astype(F32)
    dots = lax.all_to_all(dots, ("prompt", "z"), 0, 0, tiled=True)
    w_part = swap(w_part)
    query_grad = join(
        core,
        query_grad,
        query_sib,
        (2,),
        (1, HD, GROUP * HD // 2),
        lambda i, c: (0, 0, 2 * (1 - c[0]) + i),
        lambda i, c: (0, 0, i),
        "join_query",
    )
    w_down_grad = join(
        core,
        w_down_grad,
        w_part,
        (2,),
        (2, HALF, WID),
        lambda e, c: (e, 1 - c[0], 0),
        lambda e, c: (e, 0, 0),
        "join_down",
    )
    kv_mine, kv_back = kv_sum[:, :HD], swap(kv_sum[:, HD:])
    prompt_kv_grad = jnp.where(
        c == 0,
        jnp.concatenate([kv_mine, kv_back], axis=2),
        jnp.concatenate([kv_back, kv_mine], axis=2),
    )[None]
    dots, query_grad, w_down_grad = lax.optimization_barrier((dots, query_grad, w_down_grad))
    route_grad = collect(slot, weight_cols, dots).T
    return (query_grad, prompt_kv_grad, w_down_grad, route_grad)


def solution(mesh):
    cores = Mesh(mesh.devices.reshape(NP, NZ, 2), ("prompt", "z", "c"))
    member = ("z", "c")
    return jax.shard_map(
        body,
        mesh=cores,
        in_specs=(
            P("prompt", member, None),
            P("prompt", member, None),
            P("prompt", None, member),
            P("prompt", None, member),
            P("prompt", None, member, None),
            P("prompt", member),
            P("prompt", None, None),
            P("prompt", None),
            P("prompt", None),
            P("prompt", None, member),
        ),
        out_specs=(
            P("prompt", member, None),
            P("prompt", None, member, None),
            P("prompt", None, member),
            P("prompt", None),
        ),
        check_vma=False,
    )
```

time: 307 us -> 140 us (0.46)
  matrix products: 79.2 us -> 0 us
  Pallas kernels: 0 us -> 51.9 us
  blocking collectives: 48.5 us -> 0 us
  local copies, waits for them, and re-layouts: 48.5 us -> 4.94 us
  other arithmetic: 38.3 us -> 4.29 us
  starting transfers between devices: 25.8 us -> 40.4 us
  waiting for transfers between devices: 50.8 us -> 36.9 us
  between operations: 14.3 us -> 0.82 us
    dot_general x7 -> x0, matrix products: 79.2 us -> none  [the longest x1 20.4 us: attend_piece(): jnp.einsum('rkgd,nkd->kgrn', grad_heads, value_heads, preferred_element_t...]
    pallas_call x0 -> x8, Pallas kernels: none -> 51.9 us  [the longest x3 32.3 us: attend(): pl.pallas_call(functools.partial(attend_kernel, first, last), out_shape=t...]
    psum x1 -> x0, blocking collectives: 48.5 us -> none  [body(): route_grad = lax.psum(route_part, 'member')]
    another operation x3 -> x0, other arithmetic: 35.3 us -> none
    ppermute x0 -> x19, waiting for transfers between devices: none -> 29.2 us  [the longest x8 23.5 us: across(): return lax.ppermute(x, 'z', [(i, i ^ by) for i in range(NZ)])]
    ppermute x0 -> x19, starting transfers between devices: none -> 24.8 us  [the longest x8 17.7 us: across(): return lax.ppermute(x, 'z', [(i, i ^ by) for i in range(NZ)])]
    all_to_all x4 -> x2, waiting for transfers between devices: 31.8 us -> 7.74 us  [the longest x1 7.74 us: body(): dots = lax.all_to_all(dots, ('prompt', 'z'), 0, 0, tiled=True)]
    scatter x3 -> x0, local copies, waits for them, and re-layouts: 22.8 us -> none  [the longest x1 9.15 us: body(): spread_hidden = jnp.zeros((slot_total, EFF), jnp.bfloat16).at[slot_index]...]
  transfers between devices with their start and end apart: 6 -> 21, of which waited for: 2 -> 11; matrix products, arithmetic and copies ran while one was open for 53% -> 5% of each run, Pallas kernels for 0% -> 30%
where the time goes in v1:
time: 140 us; the launch traced here: 139 us
  Pallas kernels  51.9 us (37%)
  starting transfers between devices  40.4 us (29%)
  waiting for transfers between devices  36.9 us (26%)
  local copies, waits for them, and re-layouts  4.94 us (4%)
  other arithmetic  4.29 us (3%)
    pallas_call x3, Pallas kernels, attend(): pl.pallas_call(functools.partial(attend_kernel, first, last), out_shape=t...  32.3 us
    ppermute x8, waiting for transfers between devices, across(): return lax.ppermute(x, 'z', [(i, i ^ by) for i in range(NZ)])  23.5 us
    ppermute x8, starting transfers between devices, across(): return lax.ppermute(x, 'z', [(i, i ^ by) for i in range(NZ)])  17.7 us
    all_to_all x1, starting transfers between devices, body(): dots = lax.all_to_all(dots, ('prompt', 'z'), 0, 0, tiled=True)  10.4 us
    all_to_all x1, waiting for transfers between devices, body(): dots = lax.all_to_all(dots, ('prompt', 'z'), 0, 0, tiled=True)  7.74 us
    pallas_call x1, Pallas kernels, dispatch(): pl.pallas_call(dispatch_kernel, out_shape=(jax.ShapeDtypeStruct((NP, SLOT...  7.59 us
    pallas_call x1, Pallas kernels, experts(): pl.pallas_call(expert_kernel, out_shape=(jax.ShapeDtypeStruct((LOCAL, 1,...  7.39 us
    ppermute x11, starting transfers between devices, swap(): return lax.ppermute(x, 'c', SWAP)  7.15 us
  transfers between devices with their start and end apart: 21, of which 11 were waited for; matrix products, arithmetic and copies ran while one was open for 5% of the time, Pallas kernels for 30%

profile of v1, /device:TPU:1, one launch (start us, length us, event | category | flops | bytes accessed | tf_op | source)
XLA Modules:
  0.0 139.2 jit_solution(17722424568912776034)
XLA Ops:
  0.6 3.3 %collective-permute-start = (bf16[1,128,4096]{2,1,0:T(8,128)(2,1)}, bf16[1,128,4096]{2,1,0:T(8,128)(2,1)S(1)}, u32[]{:S(2)}, u32[]{:S(2)}) collective-permute-start(bf16[1,128,4096]{2,1,0:T(8,128)(2,1)} %refs_1_.5), channel_id=1, source_target_pairs={{0,1},{1,0},{2,3},{3,2},{4,5},{5,4},{6,7},{7,6},{8,9},{9,8},{10,11... | collective-permute-start | bytes 3145736 | tf_op jit(solution)/shard_map/ppermute | solution.py:327
  4.0 0.1 collective-permute-start.1
  4.1 0.4 collective-permute-start.2
  4.5 0.1 collective-permute-start.3
  4.6 0.4 collective-permute-start.4
  5.0 7.6 %dispatch.1 = (bf16[16,128,1024]{2,1,0:T(8,128)(2,1)}, s32[8,128]{1,0:T(8,128)}, bf16[4,768,256]{2,1,0:T(8,128)(2,1)}) custom-call(s32[1]{0:T(128)} %bitcast.c_ref.refs_0_, s32[8,128]{1,0:T(8,128)} %bitcast.41, f32[8,128]{1,0:T(8,128)} %bitcast.36, bf16[128,256]{1,0:T(8,128)(2,1)} %grad_ref.1, bf16[1024,1536]{1,0:T(8,128)(2,1)} %bitcast.39, ...), custom_call_target="tpu_custom_call" | custom-call | flops 3221225472 | bytes 6291456 | tf_op jit(solution)/shard_map/dispatch/pallas_call | solution.py:94
  12.6 0.0 collective-permute-done.4
  12.6 0.0 collective-permute-done.2.refs_6_
  12.7 0.0 collective-permute-done.3.refs_8_
  12.7 0.0 collective-permute-done.refs_2_
  12.7 0.0 collective-permute-done.1.refs_4_
  12.7 1.0 copy-done.5
  13.7 0.3 copy-done.4
  14.0 5.2 %all-to-all-start = ((bf16[16,128,1024]{2,1,0:T(8,128)(2,1)}), bf16[16,128,1024]{2,1,0:T(8,128)(2,1)}, u32[]{:S(2)}, u32[]{:S(2)}) async-start(bf16[16,128,1024]{2,1,0:T(8,128)(2,1)} %get-tuple-element.35), calls=%async_computation | async-start | bytes 8388608 | tf_op jit(solution)/shard_map/all_to_all | solution.py:342
  19.3 6.1 %collective-permute-start.7 = (bf16[1,2,256,128]{3,2,1,0:T(8,128)(2,1)S(1)}, bf16[1,2,256,128]{3,2,1,0:T(8,128)(2,1)S(1)}, u32[]{:S(2)}, u32[]{:S(2)}) collective-permute-start(bf16[1,2,256,128]{3,2,1,0:T(8,128)(2,1)S(1)} %fusion.6), channel_id=1, source_target_pairs={{0,12},{2,14},{4,8},{6,10},{8,4},{10,6},{12,0},{14,2},{1,13},{3,15... | collective-permute-start | bytes 393224 | tf_op jit(solution)/shard_map/ppermute | solution.py:330
  25.4 1.2 collective-permute-start.6
  26.6 1.0 collective-permute-start.5
  27.6 0.9 collective-permute-start.14
  28.5 3.0 %collective-permute-done.7 = bf16[1,2,256,128]{3,2,1,0:T(8,128)(2,1)S(1)} collective-permute-done((bf16[1,2,256,128]{3,2,1,0:T(8,128)(2,1)S(1)}, bf16[1,2,256,128]{3,2,1,0:T(8,128)(2,1)S(1)}, u32[]{:S(2)}, u32[]{:S(2)}) %collective-permute-start.7) | collective-permute-done | bytes 131104 | tf_op jit(solution)/shard_map/ppermute | solution.py:330
  31.5 1.6 %collective-permute-done.6 = bf16[1,2,256,128]{3,2,1,0:T(8,128)(2,1)S(1)} collective-permute-done((bf16[1,2,256,128]{3,2,1,0:T(8,128)(2,1)S(1)}, bf16[1,2,256,128]{3,2,1,0:T(8,128)(2,1)S(1)}, u32[]{:S(2)}, u32[]{:S(2)}) %collective-permute-start.6) | collective-permute-done | bytes 131104 | tf_op jit(solution)/shard_map/ppermute | solution.py:330
  33.1 5.7 %collective-permute-done.5 = bf16[1,2,256,128]{3,2,1,0:T(8,128)(2,1)S(1)} collective-permute-done((bf16[1,2,256,128]{3,2,1,0:T(8,128)(2,1)S(1)}, bf16[1,2,256,128]{3,2,1,0:T(8,128)(2,1)S(1)}, u32[]{:S(2)}, u32[]{:S(2)}) %collective-permute-start.5) | collective-permute-done | bytes 131104 | tf_op jit(solution)/shard_map/ppermute | solution.py:330
  38.8 0.1 pad_maximum_fusion
  38.9 0.5 collective-permute-start.8
  39.3 0.7 pad_maximum_fusion.1.refs_9_
  40.1 8.9 %attend_2.2 = (f32[2,2,256,128]{3,2,1,0:T(8,128)}, f32[256,2048]{1,0:T(8,128)}) custom-call(s32[1]{0:T(128)} %bitcast.c_ref.refs_0_, bf16[1,128,4096]{2,1,0:T(8,128)(2,1)} %refs_1_.5, bf16[1,128,4096]{2,1,0:T(8,128)(2,1)} %copy-done.4, bf16[1,128,4096]{2,1,0:T(8,128)(2,1)} %refs_3_.5, bf16[1,128,4096]{2,1,0:T(8,128)(2,1)} %copy-done.5, ...), custom_call_target="tpu_custom_call" | custom-call | flops 5368709120 | bytes 8388608 | tf_op jit(solution)/shard_map/attend_2/pallas_call | solution.py:269
  48.9 1.6 %collective-permute-done.8.refs_9_ = bf16[4,2,256,128]{3,2,1,0:T(8,128)(2,1)S(1)} collective-permute-done((bf16[4,2,256,128]{3,2,1,0:T(8,128)(2,1)S(1)}, bf16[4,2,256,128]{3,2,1,0:T(8,128)(2,1)S(1)}, u32[]{:S(2)}, u32[]{:S(2)}) %collective-permute-start.8) | collective-permute-done | bytes 524320 | tf_op jit(solution)/shard_map/ppermute | solution.py:330
  50.6 0.8 copy-done.7
  51.4 14.3 %attend_4.1 = (bf16[4,2,256,128]{3,2,1,0:T(8,128)(2,1)}, f32[256,2048]{1,0:T(8,128)}) custom-call(s32[1]{0:T(128)} %bitcast.c_ref.refs_0_, bf16[1,128,4096]{2,1,0:T(8,128)(2,1)} %refs_1_.5, bf16[1,128,4096]{2,1,0:T(8,128)(2,1)} %copy-done.4, bf16[1,128,4096]{2,1,0:T(8,128)(2,1)} %refs_3_.5, bf16[1,128,4096]{2,1,0:T(8,128)(2,1)} %copy-done.5, ...), custom_call_target="tpu_custom_call" | custom-call | flops 10737418240 | bytes 8388608 | tf_op jit(solution)/shard_map/attend_4/pallas_call | solution.py:269
  65.7 1.1 collective-permute-start.9
  66.8 0.7 pad_maximum_fusion.2.refs_9_
  67.5 9.1 %attend_2.3 = (f32[2,2,256,128]{3,2,1,0:T(8,128)}, bf16[1,128,4096]{2,1,0:T(8,128)(2,1)}, bf16[128,2048]{1,0:T(8,128)(2,1)}) custom-call(s32[1]{0:T(128)} %bitcast.c_ref.refs_0_, bf16[1,128,4096]{2,1,0:T(8,128)(2,1)} %refs_1_.5, bf16[1,128,4096]{2,1,0:T(8,128)(2,1)} %copy-done.4, bf16[1,128,4096]{2,1,0:T(8,128)(2,1)} %refs_3_.5, ...), custom_call_target="tpu_custom_call" | custom-call | flops 5368709120 | bytes 8388608 | tf_op jit(solution)/shard_map/attend_2/pallas_call | solution.py:269
  76.6 0.2 collective-permute-done.9
  76.8 0.1 convert_element_type.19
  76.9 1.2 fusion
  78.1 3.2 %collective-permute-start.10 = (bf16[2,256,128]{2,1,0:T(8,128)(2,1)S(1)}, bf16[2,256,128]{2,1,0:T(8,128)(2,1)S(1)}, u32[]{:S(2)}, u32[]{:S(2)}) collective-permute-start(bf16[2,256,128]{2,1,0:T(8,128)(2,1)S(1)} %fusion.7), channel_id=1, source_target_pairs={{0,8},{2,10},{4,12},{6,14},{8,0},{10,2},{12,4},{14,6},{1,9},{3,11}... | collective-permute-start | bytes 393224 | tf_op jit(solution)/shard_map/ppermute | solution.py:330
  81.3 4.5 %collective-permute-start.12 = (bf16[2,256,128]{2,1,0:T(8,128)(2,1)S(1)}, bf16[2,256,128]{2,1,0:T(8,128)(2,1)S(1)}, u32[]{:S(2)}, u32[]{:S(2)}) collective-permute-start(bf16[2,256,128]{2,1,0:T(8,128)(2,1)S(1)} %get-tuple-element.68), channel_id=1, source_target_pairs={{0,12},{2,14},{4,8},{6,10},{8,4},{10,6},{12,0},{14,2},{1,13},{3,15... | collective-permute-start | bytes 393224 | tf_op jit(solution)/shard_map/ppermute | solution.py:330
  85.8 0.0 collective-permute-start.11
  85.8 0.1 collective-permute-done.10
  85.9 9.6 %collective-permute-done.12 = bf16[2,256,128]{2,1,0:T(8,128)(2,1)S(1)} collective-permute-done((bf16[2,256,128]{2,1,0:T(8,128)(2,1)S(1)}, bf16[2,256,128]{2,1,0:T(8,128)(2,1)S(1)}, u32[]{:S(2)}, u32[]{:S(2)}) %collective-permute-start.12) | collective-permute-done | bytes 131104 | tf_op jit(solution)/shard_map/ppermute | solution.py:330
  95.6 1.7 %collective-permute-done.11 = bf16[2,256,128]{2,1,0:T(8,128)(2,1)S(1)} collective-permute-done((bf16[2,256,128]{2,1,0:T(8,128)(2,1)S(1)}, bf16[2,256,128]{2,1,0:T(8,128)(2,1)S(1)}, u32[]{:S(2)}, u32[]{:S(2)}) %collective-permute-start.11) | collective-permute-done | bytes 131104 | tf_op jit(solution)/shard_map/ppermute | solution.py:330
  97.2 0.0 all-to-all-done.got_ref
  97.2 1.3 slice.41
  98.6 0.7 collective-permute-start.13
  99.2 0.0 collective-permute-done.14.wsib_ref
  99.2 2.4 %collective-permute-done.13.ssib_ref = bf16[16,128,256]{2,1,0:T(8,128)(2,1)} collective-permute-done((bf16[16,128,256]{2,1,0:T(8,128)(2,1)S(1)}, bf16[16,128,256]{2,1,0:T(8,128)(2,1)}, u32[]{:S(2)}, u32[]{:S(2)}) %collective-permute-start.13) | collective-permute-done | bytes 1048608 | tf_op jit(solution)/shard_map/ppermute | solution.py:327
  101.7 7.4 %experts.1 = (f32[4,1,512]{2,1,0:T(1,128)}, bf16[4,1536,256]{2,1,0:T(8,128)(2,1)}, bf16[4,768,256]{2,1,0:T(8,128)(2,1)}) custom-call(s32[1]{0:T(128)} %bitcast.c_ref.refs_0_, bf16[16,128,1024]{2,1,0:T(8,128)(2,1)} %all-to-all-done.got_ref, bf16[16,128,256]{2,1,0:T(8,128)(2,1)} %collective-permute-done.13.ssib_ref, bf16[4,1536,256]{2,1,0:T(8,128)(2,1)} %wown_ref.1, ...), custom_call_target="tpu_custom_call" | custom-call | flops 3221225472 | bytes 13631488 | tf_op jit(solution)/shard_map/experts/pallas_call | solution.py:140
  109.0 0.4 collective-permute-start.17
  109.4 0.1 collective-permute-start.16
  109.6 0.1 fusion.3
  109.6 0.5 collective-permute-start.15
  110.1 0.2 collective-permute-start.18
  110.3 3.3 %collective-permute-done.15 = f32[4,1,512]{2,1,0:T(1,128)S(1)} collective-permute-done((f32[4,1,512]{2,1,0:T(1,128)}, f32[4,1,512]{2,1,0:T(1,128)S(1)}, u32[]{:S(2)}, u32[]{:S(2)}) %collective-permute-start.15) | collective-permute-done | bytes 8224 | tf_op jit(solution)/shard_map/ppermute | solution.py:327
  113.6 0.7 add_reduce_fusion
  114.3 0.1 reshape.77
  114.4 0.1 broadcast_in_dim.19
  114.5 0.6 broadcast_in_dim.20
  115.2 10.4 %all-to-all-start.1 = ((f32[128,1,128]{2,1,0:T(1,128)}), f32[128,1,128]{2,1,0:T(1,128)S(1)}, u32[]{:S(2)}, u32[]{:S(2)}) async-start(f32[128,1,128]{2,1,0:T(1,128)} %bitcast.10), calls=%async_computation.1 | async-start | bytes 131072 | tf_op jit(solution)/shard_map/all_to_all | solution.py:371
  125.6 0.7 maximum_select_fusion
  126.3 0.9 join_query.1
  127.1 0.0 collective-permute-done.17.part_ref
  127.2 1.2 join_down.1
  128.3 7.7 %all-to-all-done.1 = f32[128,1,128]{2,1,0:T(1,128)S(1)} async-done(((f32[128,1,128]{2,1,0:T(1,128)}), f32[128,1,128]{2,1,0:T(1,128)S(1)}, u32[]{:S(2)}, u32[]{:S(2)}) %all-to-all-start.1) | async-done | bytes 65568 | tf_op jit(solution)/shard_map/all_to_all | solution.py:371
  136.1 0.6 copy-done.1
  136.7 2.5 %collect.1 = f32[8,128]{1,0:T(8,128)} custom-call(s32[8,128]{1,0:T(8,128)} %get-tuple-element.62.slot_ref, f32[8,128]{1,0:T(8,128)} %bitcast.37, f32[128,128]{1,0:T(8,128)} %bitcast.31), custom_call_target="tpu_custom_call" | custom-call | flops 8388608 | bytes 262144 | tf_op jit(solution)/shard_map/collect/pallas_call | solution.py:301
  (23 shorter events, 0.1 us)
Async XLA Ops:
  0.6 12.1 %collective-permute-start = (bf16[1,128,4096]{2,1,0:T(8,128)(2,1)}, bf16[1,128,4096]{2,1,0:T(8,128)(2,1)S(1)}, u32[]{:S(2)}, u32[]{:S(2)}) collective-permute-start(bf16[1,128,4096]{2,1,0:T(8,128)(2,1)} %refs_1_.5), channel_id=1, source_target_pairs={{0,1},{1,0},{2,3},{3,2},{4,5},{5,4},{6,7},{7,6},{8,9},{9,8},{10,11... | collective-permute-start | bytes 3145736 | tf_op jit(solution)/shard_map/ppermute | solution.py:327
  4.0 8.7 %collective-permute-start.1 = (bf16[1,128,4096]{2,1,0:T(8,128)(2,1)}, bf16[1,128,4096]{2,1,0:T(8,128)(2,1)S(1)}, u32[]{:S(2)}, u32[]{:S(2)}) collective-permute-start(bf16[1,128,4096]{2,1,0:T(8,128)(2,1)} %refs_3_.5), channel_id=1, source_target_pairs={{0,1},{1,0},{2,3},{3,2},{4,5},{5,4},{6,7},{7,6},{8,9},{9,8},{10,11... | collective-permute-start | bytes 3145736 | tf_op jit(solution)/shard_map/ppermute | solution.py:327
  4.1 8.6 %collective-permute-start.2 = (f32[1,32,128]{2,1,0:T(8,128)}, f32[1,32,128]{2,1,0:T(8,128)S(1)}, u32[]{:S(2)}, u32[]{:S(2)}) collective-permute-start(f32[1,32,128]{2,1,0:T(8,128)} %refs_5_.5), channel_id=1, source_target_pairs={{0,1},{1,0},{2,3},{3,2},{4,5},{5,4},{6,7},{7,6},{8,9},{9,8},{10,11... | collective-permute-start | bytes 49160 | tf_op jit(solution)/shard_map/ppermute | solution.py:327
  4.5 8.2 %collective-permute-start.3 = (f32[1,32,128]{2,1,0:T(8,128)}, f32[1,32,128]{2,1,0:T(8,128)S(1)}, u32[]{:S(2)}, u32[]{:S(2)}) collective-permute-start(f32[1,32,128]{2,1,0:T(8,128)} %refs_7_.5), channel_id=1, source_target_pairs={{0,1},{1,0},{2,3},{3,2},{4,5},{5,4},{6,7},{7,6},{8,9},{9,8},{10,11... | collective-permute-start | bytes 49160 | tf_op jit(solution)/shard_map/ppermute | solution.py:327
  4.6 8.0 %collective-permute-start.4 = (bf16[2,128,256]{2,1,0:T(8,128)(2,1)}, bf16[2,128,256]{2,1,0:T(8,128)(2,1)S(1)}, u32[]{:S(2)}, u32[]{:S(2)}) collective-permute-start(bf16[2,128,256]{2,1,0:T(8,128)(2,1)} %bitcast.34), channel_id=1, source_target_pairs={{0,1},{1,0},{2,3},{3,2},{4,5},{5,4},{6,7},{7,6},{8,9},{9,8},{10,11... | collective-permute-start | bytes 393224 | tf_op jit(solution)/shard_map/ppermute | solution.py:327
  5.0 7.6 %copy-start.2 = (bf16[1,2,128,256]{3,2,1,0:T(8,128)(2,1)S(1)}, bf16[1,2,128,256]{3,2,1,0:T(8,128)(2,1)}, u32[]{:S(2)}) copy-start(bf16[1,2,128,256]{3,2,1,0:T(8,128)(2,1)} %param.14) | copy-start | bytes 393220
  12.7 27.4 %copy-start.8 = (f32[1,32,128]{2,1,0:T(8,128)}, f32[1,32,128]{2,1,0:T(8,128)S(1)}, u32[]{:S(2)}) copy-start(f32[1,32,128]{2,1,0:T(8,128)S(1)} %collective-permute-done.2.refs_6_) | copy-start | bytes 49156
  12.7 27.4 %copy-start.9 = (f32[1,32,128]{2,1,0:T(8,128)}, f32[1,32,128]{2,1,0:T(8,128)S(1)}, u32[]{:S(2)}) copy-start(f32[1,32,128]{2,1,0:T(8,128)S(1)} %collective-permute-done.3.refs_8_) | copy-start | bytes 49156
  12.7 1.4 copy-start.4
  12.7 1.0 copy-start.5
  13.7 13.8 %copy-start.3 = (bf16[4,768,256]{2,1,0:T(8,128)(2,1)S(1)}, bf16[4,768,256]{2,1,0:T(8,128)(2,1)}, u32[]{:S(2)}) copy-start(bf16[4,768,256]{2,1,0:T(8,128)(2,1)} %get-tuple-element.51) | copy-start | bytes 4718596
  14.0 83.2 %all-to-all-start = ((bf16[16,128,1024]{2,1,0:T(8,128)(2,1)}), bf16[16,128,1024]{2,1,0:T(8,128)(2,1)}, u32[]{:S(2)}, u32[]{:S(2)}) async-start(bf16[16,128,1024]{2,1,0:T(8,128)(2,1)} %get-tuple-element.35), calls=%async_computation | async-start | bytes 8388608 | tf_op jit(solution)/shard_map/all_to_all | solution.py:342
  19.3 12.2 %collective-permute-start.7 = (bf16[1,2,256,128]{3,2,1,0:T(8,128)(2,1)S(1)}, bf16[1,2,256,128]{3,2,1,0:T(8,128)(2,1)S(1)}, u32[]{:S(2)}, u32[]{:S(2)}) collective-permute-start(bf16[1,2,256,128]{3,2,1,0:T(8,128)(2,1)S(1)} %fusion.6), channel_id=1, source_target_pairs={{0,12},{2,14},{4,8},{6,10},{8,4},{10,6},{12,0},{14,2},{1,13},{3,15... | collective-permute-start | bytes 393224 | tf_op jit(solution)/shard_map/ppermute | solution.py:330
  25.4 7.7 %collective-permute-start.6 = (bf16[1,2,256,128]{3,2,1,0:T(8,128)(2,1)S(1)}, bf16[1,2,256,128]{3,2,1,0:T(8,128)(2,1)S(1)}, u32[]{:S(2)}, u32[]{:S(2)}) collective-permute-start(bf16[1,2,256,128]{3,2,1,0:T(8,128)(2,1)S(1)} %fusion.6), channel_id=1, source_target_pairs={{0,4},{2,6},{4,0},{6,2},{8,12},{10,14},{12,8},{14,10},{1,5},{3,7},... | collective-permute-start | bytes 393224 | tf_op jit(solution)/shard_map/ppermute | solution.py:330
  26.6 12.2 %collective-permute-start.5 = (bf16[1,2,256,128]{3,2,1,0:T(8,128)(2,1)S(1)}, bf16[1,2,256,128]{3,2,1,0:T(8,128)(2,1)S(1)}, u32[]{:S(2)}, u32[]{:S(2)}) collective-permute-start(bf16[1,2,256,128]{3,2,1,0:T(8,128)(2,1)S(1)} %fusion.6), channel_id=1, source_target_pairs={{0,8},{2,10},{4,12},{6,14},{8,0},{10,2},{12,4},{14,6},{1,9},{3,11}... | collective-permute-start | bytes 393224 | tf_op jit(solution)/shard_map/ppermute | solution.py:330
  27.6 71.7 %collective-permute-start.14 = (bf16[4,768,256]{2,1,0:T(8,128)(2,1)S(1)}, bf16[4,768,256]{2,1,0:T(8,128)(2,1)}, u32[]{:S(2)}, u32[]{:S(2)}) collective-permute-start(bf16[4,768,256]{2,1,0:T(8,128)(2,1)S(1)} %copy-done.3), channel_id=1, source_target_pairs={{0,1},{1,0},{2,3},{3,2},{4,5},{5,4},{6,7},{7,6},{8,9},{9,8},{10,11... | collective-permute-start | bytes 4718600 | tf_op jit(solution)/shard_map/ppermute | solution.py:327
  38.9 11.7 %collective-permute-start.8 = (bf16[4,2,256,128]{3,2,1,0:T(8,128)(2,1)S(1)}, bf16[4,2,256,128]{3,2,1,0:T(8,128)(2,1)S(1)}, u32[]{:S(2)}, u32[]{:S(2)}) collective-permute-start(bf16[4,2,256,128]{3,2,1,0:T(8,128)(2,1)S(1)} %pad_maximum_fusion), channel_id=1, source_target_pairs={{0,2},{2,0},{4,6},{6,4},{8,10},{10,8},{12,14},{14,12},{1,3},{3,1},... | collective-permute-start | bytes 1572872 | tf_op jit(solution)/shard_map/ppermute | solution.py:330
  50.6 0.8 copy-start.7
  65.7 11.1 %collective-permute-start.9 = (bf16[4,2,256,128]{3,2,1,0:T(8,128)(2,1)}, bf16[4,2,256,128]{3,2,1,0:T(8,128)(2,1)S(1)}, u32[]{:S(2)}, u32[]{:S(2)}) collective-permute-start(bf16[4,2,256,128]{3,2,1,0:T(8,128)(2,1)} %get-tuple-element.43), channel_id=1, source_target_pairs={{0,2},{2,0},{4,6},{6,4},{8,10},{10,8},{12,14},{14,12},{1,3},{3,1},... | collective-permute-start | bytes 1572872 | tf_op jit(solution)/shard_map/ppermute | solution.py:330
  67.5 9.3 %copy-start = (f32[2,2,256,128]{3,2,1,0:T(8,128)S(1)}, f32[2,2,256,128]{3,2,1,0:T(8,128)}, u32[]{:S(2)}) copy-start(f32[2,2,256,128]{3,2,1,0:T(8,128)} %get-tuple-element.46) | copy-start | bytes 1572868
  78.1 7.9 %collective-permute-start.10 = (bf16[2,256,128]{2,1,0:T(8,128)(2,1)S(1)}, bf16[2,256,128]{2,1,0:T(8,128)(2,1)S(1)}, u32[]{:S(2)}, u32[]{:S(2)}) collective-permute-start(bf16[2,256,128]{2,1,0:T(8,128)(2,1)S(1)} %fusion.7), channel_id=1, source_target_pairs={{0,8},{2,10},{4,12},{6,14},{8,0},{10,2},{12,4},{14,6},{1,9},{3,11}... | collective-permute-start | bytes 393224 | tf_op jit(solution)/shard_map/ppermute | solution.py:330
  81.3 14.2 %collective-permute-start.12 = (bf16[2,256,128]{2,1,0:T(8,128)(2,1)S(1)}, bf16[2,256,128]{2,1,0:T(8,128)(2,1)S(1)}, u32[]{:S(2)}, u32[]{:S(2)}) collective-permute-start(bf16[2,256,128]{2,1,0:T(8,128)(2,1)S(1)} %get-tuple-element.68), channel_id=1, source_target_pairs={{0,12},{2,14},{4,8},{6,10},{8,4},{10,6},{12,0},{14,2},{1,13},{3,15... | collective-permute-start | bytes 393224 | tf_op jit(solution)/shard_map/ppermute | solution.py:330
  85.8 11.4 %collective-permute-start.11 = (bf16[2,256,128]{2,1,0:T(8,128)(2,1)S(1)}, bf16[2,256,128]{2,1,0:T(8,128)(2,1)S(1)}, u32[]{:S(2)}, u32[]{:S(2)}) collective-permute-start(bf16[2,256,128]{2,1,0:T(8,128)(2,1)S(1)} %get-tuple-element.69), channel_id=1, source_target_pairs={{0,4},{2,6},{4,0},{6,2},{8,12},{10,14},{12,8},{14,10},{1,5},{3,7},... | collective-permute-start | bytes 393224 | tf_op jit(solution)/shard_map/ppermute | solution.py:330
  98.5 10.9 %copy-start.6 = (bf16[128,2048]{1,0:T(8,128)(2,1)S(1)}, bf16[128,2048]{1,0:T(8,128)(2,1)}, u32[]{:S(2)}) copy-start(bf16[128,2048]{1,0:T(8,128)(2,1)} %get-tuple-element.54) | copy-start | bytes 1572868
  98.6 3.1 %collective-permute-start.13 = (bf16[16,128,256]{2,1,0:T(8,128)(2,1)S(1)}, bf16[16,128,256]{2,1,0:T(8,128)(2,1)}, u32[]{:S(2)}, u32[]{:S(2)}) collective-permute-start(bf16[16,128,256]{2,1,0:T(8,128)(2,1)S(1)} %slice.41), channel_id=1, source_target_pairs={{0,1},{1,0},{2,3},{3,2},{4,5},{5,4},{6,7},{7,6},{8,9},{9,8},{10,11... | collective-permute-start | bytes 3145736 | tf_op jit(solution)/shard_map/ppermute | solution.py:327
  109.0 18.1 %collective-permute-start.17 = (bf16[4,768,256]{2,1,0:T(8,128)(2,1)}, bf16[4,768,256]{2,1,0:T(8,128)(2,1)S(1)}, u32[]{:S(2)}, u32[]{:S(2)}) collective-permute-start(bf16[4,768,256]{2,1,0:T(8,128)(2,1)} %get-tuple-element.56), channel_id=1, source_target_pairs={{0,1},{1,0},{2,3},{3,2},{4,5},{5,4},{6,7},{7,6},{8,9},{9,8},{10,11... | collective-permute-start | bytes 4718600 | tf_op jit(solution)/shard_map/ppermute | solution.py:327
  109.4 16.8 %collective-permute-start.16 = (bf16[1,128,2048]{2,1,0:T(8,128)(2,1)S(1)}, bf16[1,128,2048]{2,1,0:T(8,128)(2,1)S(1)}, u32[]{:S(2)}, u32[]{:S(2)}) collective-permute-start(bf16[1,128,2048]{2,1,0:T(8,128)(2,1)S(1)} %bitcast.40), channel_id=1, source_target_pairs={{0,1},{1,0},{2,3},{3,2},{4,5},{5,4},{6,7},{7,6},{8,9},{9,8},{10,11... | collective-permute-start | bytes 1572872 | tf_op jit(solution)/shard_map/ppermute | solution.py:327
  109.6 4.0 %collective-permute-start.15 = (f32[4,1,512]{2,1,0:T(1,128)}, f32[4,1,512]{2,1,0:T(1,128)S(1)}, u32[]{:S(2)}, u32[]{:S(2)}) collective-permute-start(f32[4,1,512]{2,1,0:T(1,128)} %get-tuple-element.52), channel_id=1, source_target_pairs={{0,1},{1,0},{2,3},{3,2},{4,5},{5,4},{6,7},{7,6},{8,9},{9,8},{10,11... | collective-permute-start | bytes 24584 | tf_op jit(solution)/shard_map/ppermute | solution.py:327
  110.1 15.4 %collective-permute-start.18 = (f32[2,128,128]{2,1,0:T(8,128)S(1)}, f32[2,128,128]{2,1,0:T(8,128)S(1)}, u32[]{:S(2)}, u32[]{:S(2)}) collective-permute-start(f32[2,128,128]{2,1,0:T(8,128)S(1)} %get-tuple-element.67), channel_id=1, source_target_pairs={{0,1},{1,0},{2,3},{3,2},{4,5},{5,4},{6,7},{7,6},{8,9},{9,8},{10,11... | collective-permute-start | bytes 393224 | tf_op jit(solution)/shard_map/ppermute | solution.py:327
  115.2 20.9 %all-to-all-start.1 = ((f32[128,1,128]{2,1,0:T(1,128)}), f32[128,1,128]{2,1,0:T(1,128)S(1)}, u32[]{:S(2)}, u32[]{:S(2)}) async-start(f32[128,1,128]{2,1,0:T(1,128)} %bitcast.10), calls=%async_computation.1 | async-start | bytes 131072 | tf_op jit(solution)/shard_map/all_to_all | solution.py:371
  136.1 0.6 copy-start.1

commit v2 on v1

--- a/solution.py
+++ b/solution.py
@@ -285,7 +285,7 @@
 
 
 def collect_kernel(slot_ref, w_ref, got_ref, out_ref):
-    turned = jnp.sum(got_ref[...].reshape(NP, NZ, SLOTS), axis=1).T
+    turned = jnp.sum(got_ref[...].reshape(NP, 2 * NZ, SLOTS), axis=1).T
     for k in range(TOPK):
         slot = slot_ref[k : k + 1, :]
         total = jnp.zeros((8, TOK), F32)
@@ -353,23 +353,23 @@
     kv_a, kv_b, kv_c = lax.optimization_barrier((kv_a, kv_b, kv_c))
     kv_b = kv_b.astype(F32)
     kv_a, kv_c = kv_a + kv_b[:2], (kv_c + kv_b[2:]).astype(BF)
+    got, kv_a, kv_c, query_sib = lax.optimization_barrier((got, kv_a, kv_c, query_sib))
     kv_parts = [
         across(kv_a[1].astype(BF), 4),
         across(kv_c[0], 2),
         across(kv_c[1], 6),
     ]
-    got, kv_parts, query_sib = lax.optimization_barrier((got, kv_parts, query_sib))
     query_sib = swap(query_sib[None])
 
     dots, w_down_grad, w_part = experts(core, got, swap(got[:, :, HALF:]), w_down, w_sib)
-    dots = dots + swap(dots)
     dots = jnp.transpose(dots.reshape(LOCAL, NP, CAP), (1, 0, 2)).reshape(NP, 1, SLOTS)
-    dots = jnp.broadcast_to(dots, (NP, NZ, SLOTS)).reshape(NP * NZ, SLOTS)
+    dots = jnp.broadcast_to(dots, (NP, 2 * NZ, SLOTS)).reshape(NP * 2 * NZ, SLOTS)
+    dots = lax.all_to_all(dots, ("prompt", "z", "c"), 0, 0, tiled=True)
+    w_part = swap(w_part)
+    dots, kv_parts = lax.optimization_barrier((dots, kv_parts))
     kv_sum = kv_a[0]
     for part in kv_parts:
         kv_sum = kv_sum + part.astype(F32)
-    dots = lax.all_to_all(dots, ("prompt", "z"), 0, 0, tiled=True)
-    w_part = swap(w_part)
     query_grad = join(
         core,
         query_grad,

time: 140 us -> 133 us (0.950)
  waiting for transfers between devices: 36.9 us -> 25.6 us
  starting transfers between devices: 40.4 us -> 44.5 us
    all_to_all x1, waiting for transfers between devices: 7.74 us -> 0.01 us  [body(): dots = lax.all_to_all(dots, ('prompt', 'z', 'c'), 0, 0, tiled=True)]
    ppermute x8, starting transfers between devices: 17.7 us -> 23.5 us  [across(): return lax.ppermute(x, 'z', [(i, i ^ by) for i in range(NZ)])]
    ppermute x8, waiting for transfers between devices: 23.5 us -> 18.5 us  [across(): return lax.ppermute(x, 'z', [(i, i ^ by) for i in range(NZ)])]
    all_to_all x1, waiting for transfers between devices: 0.01 us -> 4.62 us  [body(): got = lax.all_to_all(sent, 'prompt', 0, 0, tiled=True)]
    ppermute x11 -> x10, waiting for transfers between devices: 5.72 us -> 2.42 us  [swap(): return lax.ppermute(x, 'c', SWAP)]
    all_to_all x1, starting transfers between devices: 10.4 us -> 7.23 us  [body(): dots = lax.all_to_all(dots, ('prompt', 'z', 'c'), 0, 0, tiled=True)]
    ppermute x11 -> x10, starting transfers between devices: 7.15 us -> 8.65 us  [swap(): return lax.ppermute(x, 'c', SWAP)]
    unnamed x20 -> x18, local copies, waits for them, and re-layouts: 2.77 us -> 3.09 us
  transfers between devices with their start and end apart: 21 -> 20, of which waited for: 11 -> 10; matrix products, arithmetic and copies ran while one was open for 5% -> 5% of each run, Pallas kernels for 30% -> 31%
where the time goes in v2:
time: 133 us; the launch traced here: 132 us
  Pallas kernels  51.9 us (39%)
  starting transfers between devices  44.5 us (33%)
  waiting for transfers between devices  25.6 us (19%)
  local copies, waits for them, and re-layouts  5.29 us (4%)
  other arithmetic  4.29 us (3%)
    pallas_call x3, Pallas kernels, attend(): pl.pallas_call(functools.partial(attend_kernel, first, last), out_shape=t...  32.2 us
    ppermute x8, starting transfers between devices, across(): return lax.ppermute(x, 'z', [(i, i ^ by) for i in range(NZ)])  23.5 us
    ppermute x8, waiting for transfers between devices, across(): return lax.ppermute(x, 'z', [(i, i ^ by) for i in range(NZ)])  18.5 us
    ppermute x10, starting transfers between devices, swap(): return lax.ppermute(x, 'c', SWAP)  8.65 us
    pallas_call x1, Pallas kernels, dispatch(): pl.pallas_call(dispatch_kernel, out_shape=(jax.ShapeDtypeStruct((NP, SLOT...  7.59 us
    pallas_call x1, Pallas kernels, experts(): pl.pallas_call(expert_kernel, out_shape=(jax.ShapeDtypeStruct((LOCAL, 1,...  7.39 us
    all_to_all x1, starting transfers between devices, body(): dots = lax.all_to_all(dots, ('prompt', 'z', 'c'), 0, 0, tiled=True)  7.23 us
    all_to_all x1, starting transfers between devices, body(): got = lax.all_to_all(sent, 'prompt', 0, 0, tiled=True)  5.09 us
  transfers between devices with their start and end apart: 20, of which 10 were waited for; matrix products, arithmetic and copies ran while one was open for 5% of the time, Pallas kernels for 31%

profile of v2, /device:TPU:1, one launch (start us, length us, event | category | flops | bytes accessed | tf_op | source)
XLA Modules:
  0.0 132.3 jit_solution(6354680526311744131)
XLA Ops:
  0.6 3.3 %collective-permute-start = (bf16[1,128,4096]{2,1,0:T(8,128)(2,1)}, bf16[1,128,4096]{2,1,0:T(8,128)(2,1)S(1)}, u32[]{:S(2)}, u32[]{:S(2)}) collective-permute-start(bf16[1,128,4096]{2,1,0:T(8,128)(2,1)} %refs_1_.5), channel_id=1, source_target_pairs={{0,1},{1,0},{2,3},{3,2},{4,5},{5,4},{6,7},{7,6},{8,9},{9,8},{10,11... | collective-permute-start | bytes 3145736 | tf_op jit(solution)/shard_map/ppermute | solution.py:327
  4.0 0.1 collective-permute-start.1
  4.1 0.4 collective-permute-start.2
  4.5 0.1 collective-permute-start.3
  4.6 0.4 collective-permute-start.4
  5.0 7.6 %dispatch.1 = (bf16[16,128,1024]{2,1,0:T(8,128)(2,1)}, s32[8,128]{1,0:T(8,128)}, bf16[4,768,256]{2,1,0:T(8,128)(2,1)}) custom-call(s32[1]{0:T(128)} %bitcast.c_ref.refs_0_, s32[8,128]{1,0:T(8,128)} %bitcast.39, f32[8,128]{1,0:T(8,128)} %bitcast.34, bf16[128,256]{1,0:T(8,128)(2,1)} %grad_ref.1, bf16[1024,1536]{1,0:T(8,128)(2,1)} %bitcast.37, ...), custom_call_target="tpu_custom_call" | custom-call | flops 3221225472 | bytes 6291456 | tf_op jit(solution)/shard_map/dispatch/pallas_call | solution.py:94
  12.6 0.0 collective-permute-done.4
  12.6 0.0 collective-permute-done.2.refs_6_
  12.7 0.0 collective-permute-done.3.refs_8_
  12.7 0.0 collective-permute-done.refs_2_
  12.7 0.0 collective-permute-done.1.refs_4_
  12.7 0.5 copy-done.7
  13.2 0.0 copy-done.8
  13.3 0.4 copy-done.3
  13.7 0.4 copy-done.4
  14.0 5.1 %all-to-all-start = ((bf16[16,128,1024]{2,1,0:T(8,128)(2,1)}), bf16[16,128,1024]{2,1,0:T(8,128)(2,1)}, u32[]{:S(2)}, u32[]{:S(2)}) async-start(bf16[16,128,1024]{2,1,0:T(8,128)(2,1)} %get-tuple-element.38), calls=%async_computation | async-start | bytes 8388608 | tf_op jit(solution)/shard_map/all_to_all | solution.py:342
  19.1 6.1 %collective-permute-start.7 = (bf16[1,2,256,128]{3,2,1,0:T(8,128)(2,1)S(1)}, bf16[1,2,256,128]{3,2,1,0:T(8,128)(2,1)S(1)}, u32[]{:S(2)}, u32[]{:S(2)}) collective-permute-start(bf16[1,2,256,128]{3,2,1,0:T(8,128)(2,1)S(1)} %fusion.5), channel_id=1, source_target_pairs={{0,12},{2,14},{4,8},{6,10},{8,4},{10,6},{12,0},{14,2},{1,13},{3,15... | collective-permute-start | bytes 393224 | tf_op jit(solution)/shard_map/ppermute | solution.py:330
  25.2 1.2 collective-permute-start.6
  26.4 1.0 collective-permute-start.5
  27.4 0.9 collective-permute-start.11
  28.3 3.0 %collective-permute-done.7 = bf16[1,2,256,128]{3,2,1,0:T(8,128)(2,1)S(1)} collective-permute-done((bf16[1,2,256,128]{3,2,1,0:T(8,128)(2,1)S(1)}, bf16[1,2,256,128]{3,2,1,0:T(8,128)(2,1)S(1)}, u32[]{:S(2)}, u32[]{:S(2)}) %collective-permute-start.7) | collective-permute-done | bytes 131104 | tf_op jit(solution)/shard_map/ppermute | solution.py:330
  31.3 1.6 %collective-permute-done.6 = bf16[1,2,256,128]{3,2,1,0:T(8,128)(2,1)S(1)} collective-permute-done((bf16[1,2,256,128]{3,2,1,0:T(8,128)(2,1)S(1)}, bf16[1,2,256,128]{3,2,1,0:T(8,128)(2,1)S(1)}, u32[]{:S(2)}, u32[]{:S(2)}) %collective-permute-start.6) | collective-permute-done | bytes 131104 | tf_op jit(solution)/shard_map/ppermute | solution.py:330
  32.9 5.7 %collective-permute-done.5 = bf16[1,2,256,128]{3,2,1,0:T(8,128)(2,1)S(1)} collective-permute-done((bf16[1,2,256,128]{3,2,1,0:T(8,128)(2,1)S(1)}, bf16[1,2,256,128]{3,2,1,0:T(8,128)(2,1)S(1)}, u32[]{:S(2)}, u32[]{:S(2)}) %collective-permute-start.5) | collective-permute-done | bytes 131104 | tf_op jit(solution)/shard_map/ppermute | solution.py:330
  38.6 0.1 pad_maximum_fusion
  38.7 0.5 collective-permute-start.8
  39.2 0.7 pad_maximum_fusion.1.refs_9_
  39.9 8.8 %attend_2.2 = (f32[2,2,256,128]{3,2,1,0:T(8,128)}, f32[256,2048]{1,0:T(8,128)}) custom-call(s32[1]{0:T(128)} %bitcast.c_ref.refs_0_, bf16[1,128,4096]{2,1,0:T(8,128)(2,1)} %refs_1_.5, bf16[1,128,4096]{2,1,0:T(8,128)(2,1)} %copy-done.3, bf16[1,128,4096]{2,1,0:T(8,128)(2,1)} %refs_3_.5, bf16[1,128,4096]{2,1,0:T(8,128)(2,1)} %copy-done.4, ...), custom_call_target="tpu_custom_call" | custom-call | flops 5368709120 | bytes 8388608 | tf_op jit(solution)/shard_map/attend_2/pallas_call | solution.py:269
  48.7 1.7 %collective-permute-done.8.refs_9_ = bf16[4,2,256,128]{3,2,1,0:T(8,128)(2,1)S(1)} collective-permute-done((bf16[4,2,256,128]{3,2,1,0:T(8,128)(2,1)S(1)}, bf16[4,2,256,128]{3,2,1,0:T(8,128)(2,1)S(1)}, u32[]{:S(2)}, u32[]{:S(2)}) %collective-permute-start.8) | collective-permute-done | bytes 524320 | tf_op jit(solution)/shard_map/ppermute | solution.py:330
  50.4 0.8 copy-done.6
  51.2 14.3 %attend_4.1 = (bf16[4,2,256,128]{3,2,1,0:T(8,128)(2,1)}, f32[256,2048]{1,0:T(8,128)}) custom-call(s32[1]{0:T(128)} %bitcast.c_ref.refs_0_, bf16[1,128,4096]{2,1,0:T(8,128)(2,1)} %refs_1_.5, bf16[1,128,4096]{2,1,0:T(8,128)(2,1)} %copy-done.3, bf16[1,128,4096]{2,1,0:T(8,128)(2,1)} %refs_3_.5, bf16[1,128,4096]{2,1,0:T(8,128)(2,1)} %copy-done.4, ...), custom_call_target="tpu_custom_call" | custom-call | flops 10737418240 | bytes 8388608 | tf_op jit(solution)/shard_map/attend_4/pallas_call | solution.py:269
  65.5 1.2 collective-permute-start.9
  66.7 0.7 pad_maximum_fusion.2.refs_9_
  67.4 9.1 %attend_2.3 = (f32[2,2,256,128]{3,2,1,0:T(8,128)}, bf16[1,128,4096]{2,1,0:T(8,128)(2,1)}, bf16[128,2048]{1,0:T(8,128)(2,1)}) custom-call(s32[1]{0:T(128)} %bitcast.c_ref.refs_0_, bf16[1,128,4096]{2,1,0:T(8,128)(2,1)} %refs_1_.5, bf16[1,128,4096]{2,1,0:T(8,128)(2,1)} %copy-done.3, bf16[1,128,4096]{2,1,0:T(8,128)(2,1)} %refs_3_.5, ...), custom_call_target="tpu_custom_call" | custom-call | flops 5368709120 | bytes 8388608 | tf_op jit(solution)/shard_map/attend_2/pallas_call | solution.py:269
  76.5 0.1 collective-permute-done.9
  76.6 0.1 convert_element_type.19
  76.7 1.2 fusion
  77.8 4.6 %all-to-all-done.got_ref = bf16[16,128,1024]{2,1,0:T(8,128)(2,1)} async-done(((bf16[16,128,1024]{2,1,0:T(8,128)(2,1)}), bf16[16,128,1024]{2,1,0:T(8,128)(2,1)}, u32[]{:S(2)}, u32[]{:S(2)}) %all-to-all-start) | async-done | bytes 4194336 | tf_op jit(solution)/shard_map/all_to_all | solution.py:342
  82.5 1.3 slice.38
  83.7 1.3 collective-permute-start.10
  85.0 2.3 %collective-permute-done.10.ssib_ref = bf16[16,128,256]{2,1,0:T(8,128)(2,1)S(1)} collective-permute-done((bf16[16,128,256]{2,1,0:T(8,128)(2,1)S(1)}, bf16[16,128,256]{2,1,0:T(8,128)(2,1)S(1)}, u32[]{:S(2)}, u32[]{:S(2)}) %collective-permute-start.10) | collective-permute-done | bytes 1048608 | tf_op jit(solution)/shard_map/ppermute | solution.py:327
  87.3 1.0 copy-done.5
  88.3 7.4 %experts.1 = (f32[4,1,512]{2,1,0:T(1,128)}, bf16[4,1536,256]{2,1,0:T(8,128)(2,1)}, bf16[4,768,256]{2,1,0:T(8,128)(2,1)}) custom-call(s32[1]{0:T(128)} %bitcast.c_ref.refs_0_, bf16[16,128,1024]{2,1,0:T(8,128)(2,1)} %all-to-all-done.got_ref, bf16[16,128,256]{2,1,0:T(8,128)(2,1)} %copy-done.5, bf16[4,1536,256]{2,1,0:T(8,128)(2,1)} %wown_ref.1, ...), custom_call_target="tpu_custom_call" | custom-call | flops 3221225472 | bytes 13631488 | tf_op jit(solution)/shard_map/experts/pallas_call | solution.py:140
  95.7 0.4 collective-permute-start.16
  96.1 7.0 %collective-permute-start.12 = (bf16[2,256,128]{2,1,0:T(8,128)(2,1)S(1)}, bf16[2,256,128]{2,1,0:T(8,128)(2,1)S(1)}, u32[]{:S(2)}, u32[]{:S(2)}) collective-permute-start(bf16[2,256,128]{2,1,0:T(8,128)(2,1)S(1)} %fusion.6), channel_id=1, source_target_pairs={{0,8},{2,10},{4,12},{6,14},{8,0},{10,2},{12,4},{14,6},{1,9},{3,11}... | collective-permute-start | bytes 393224 | tf_op jit(solution)/shard_map/ppermute | solution.py:330
  103.1 0.7 reduce
  103.8 0.1 reshape.77
  103.9 0.1 broadcast_in_dim.19
  104.0 0.7 broadcast_in_dim.20
  104.7 7.2 %all-to-all-start.1 = ((f32[256,1,128]{2,1,0:T(1,128)}), f32[256,1,128]{2,1,0:T(1,128)S(1)}, u32[]{:S(2)}, u32[]{:S(2)}) async-start(f32[256,1,128]{2,1,0:T(1,128)} %bitcast.7), calls=%async_computation.1 | async-start | bytes 262144 | tf_op jit(solution)/shard_map/all_to_all | solution.py:367
  111.9 5.0 %collective-permute-start.14 = (bf16[2,256,128]{2,1,0:T(8,128)(2,1)S(1)}, bf16[2,256,128]{2,1,0:T(8,128)(2,1)S(1)}, u32[]{:S(2)}, u32[]{:S(2)}) collective-permute-start(bf16[2,256,128]{2,1,0:T(8,128)(2,1)S(1)} %get-tuple-element.74), channel_id=1, source_target_pairs={{0,12},{2,14},{4,8},{6,10},{8,4},{10,6},{12,0},{14,2},{1,13},{3,15... | collective-permute-start | bytes 393224 | tf_op jit(solution)/shard_map/ppermute | solution.py:330
  117.0 1.5 %collective-permute-start.13 = (bf16[2,256,128]{2,1,0:T(8,128)(2,1)S(1)}, bf16[2,256,128]{2,1,0:T(8,128)(2,1)S(1)}, u32[]{:S(2)}, u32[]{:S(2)}) collective-permute-start(bf16[2,256,128]{2,1,0:T(8,128)(2,1)S(1)} %get-tuple-element.75), channel_id=1, source_target_pairs={{0,4},{2,6},{4,0},{6,2},{8,12},{10,14},{12,8},{14,10},{1,5},{3,7},... | collective-permute-start | bytes 393224 | tf_op jit(solution)/shard_map/ppermute | solution.py:330
  118.5 0.9 collective-permute-start.15
  119.4 0.0 collective-permute-done.12
  119.4 3.2 %collective-permute-done.14 = bf16[2,256,128]{2,1,0:T(8,128)(2,1)S(1)} collective-permute-done((bf16[2,256,128]{2,1,0:T(8,128)(2,1)S(1)}, bf16[2,256,128]{2,1,0:T(8,128)(2,1)S(1)}, u32[]{:S(2)}, u32[]{:S(2)}) %collective-permute-start.14) | collective-permute-done | bytes 131104 | tf_op jit(solution)/shard_map/ppermute | solution.py:330
  122.6 3.3 %collective-permute-done.13 = bf16[2,256,128]{2,1,0:T(8,128)(2,1)S(1)} collective-permute-done((bf16[2,256,128]{2,1,0:T(8,128)(2,1)S(1)}, bf16[2,256,128]{2,1,0:T(8,128)(2,1)S(1)}, u32[]{:S(2)}, u32[]{:S(2)}) %collective-permute-start.13) | collective-permute-done | bytes 131104 | tf_op jit(solution)/shard_map/ppermute | solution.py:330
  125.9 0.0 all-to-all-done.1
  125.9 0.1 fusion.2
  126.0 0.8 collective-permute-start.17
  126.8 0.0 collective-permute-done.15.part_ref
  126.8 0.9 join_query.1
  127.7 0.1 collective-permute-done.17
  127.8 0.7 maximum_select_fusion
  128.5 1.2 join_down.1
  129.7 2.6 %collect.1 = f32[8,128]{1,0:T(8,128)} custom-call(s32[8,128]{1,0:T(8,128)} %get-tuple-element.68.slot_ref, f32[8,128]{1,0:T(8,128)} %bitcast.35, f32[256,128]{1,0:T(8,128)} %bitcast.29), custom_call_target="tpu_custom_call" | custom-call | flops 8388608 | bytes 262144 | tf_op jit(solution)/shard_map/collect/pallas_call | solution.py:301
  (19 shorter events, 0.1 us)
Async XLA Ops:
  0.6 12.0 %collective-permute-start = (bf16[1,128,4096]{2,1,0:T(8,128)(2,1)}, bf16[1,128,4096]{2,1,0:T(8,128)(2,1)S(1)}, u32[]{:S(2)}, u32[]{:S(2)}) collective-permute-start(bf16[1,128,4096]{2,1,0:T(8,128)(2,1)} %refs_1_.5), channel_id=1, source_target_pairs={{0,1},{1,0},{2,3},{3,2},{4,5},{5,4},{6,7},{7,6},{8,9},{9,8},{10,11... | collective-permute-start | bytes 3145736 | tf_op jit(solution)/shard_map/ppermute | solution.py:327
  4.0 8.7 %collective-permute-start.1 = (bf16[1,128,4096]{2,1,0:T(8,128)(2,1)}, bf16[1,128,4096]{2,1,0:T(8,128)(2,1)S(1)}, u32[]{:S(2)}, u32[]{:S(2)}) collective-permute-start(bf16[1,128,4096]{2,1,0:T(8,128)(2,1)} %refs_3_.5), channel_id=1, source_target_pairs={{0,1},{1,0},{2,3},{3,2},{4,5},{5,4},{6,7},{7,6},{8,9},{9,8},{10,11... | collective-permute-start | bytes 3145736 | tf_op jit(solution)/shard_map/ppermute | solution.py:327
  4.1 8.6 %collective-permute-start.2 = (f32[1,32,128]{2,1,0:T(8,128)}, f32[1,32,128]{2,1,0:T(8,128)S(1)}, u32[]{:S(2)}, u32[]{:S(2)}) collective-permute-start(f32[1,32,128]{2,1,0:T(8,128)} %refs_5_.5), channel_id=1, source_target_pairs={{0,1},{1,0},{2,3},{3,2},{4,5},{5,4},{6,7},{7,6},{8,9},{9,8},{10,11... | collective-permute-start | bytes 49160 | tf_op jit(solution)/shard_map/ppermute | solution.py:327
  4.5 8.2 %collective-permute-start.3 = (f32[1,32,128]{2,1,0:T(8,128)}, f32[1,32,128]{2,1,0:T(8,128)S(1)}, u32[]{:S(2)}, u32[]{:S(2)}) collective-permute-start(f32[1,32,128]{2,1,0:T(8,128)} %refs_7_.5), channel_id=1, source_target_pairs={{0,1},{1,0},{2,3},{3,2},{4,5},{5,4},{6,7},{7,6},{8,9},{9,8},{10,11... | collective-permute-start | bytes 49160 | tf_op jit(solution)/shard_map/ppermute | solution.py:327
  4.6 8.0 %collective-permute-start.4 = (bf16[2,128,256]{2,1,0:T(8,128)(2,1)}, bf16[2,128,256]{2,1,0:T(8,128)(2,1)S(1)}, u32[]{:S(2)}, u32[]{:S(2)}) collective-permute-start(bf16[2,128,256]{2,1,0:T(8,128)(2,1)} %bitcast.32), channel_id=1, source_target_pairs={{0,1},{1,0},{2,3},{3,2},{4,5},{5,4},{6,7},{7,6},{8,9},{9,8},{10,11... | collective-permute-start | bytes 393224 | tf_op jit(solution)/shard_map/ppermute | solution.py:327
  5.0 7.6 %copy-start.2 = (bf16[1,2,128,256]{3,2,1,0:T(8,128)(2,1)S(1)}, bf16[1,2,128,256]{3,2,1,0:T(8,128)(2,1)}, u32[]{:S(2)}) copy-start(bf16[1,2,128,256]{3,2,1,0:T(8,128)(2,1)} %param.14) | copy-start | bytes 393220
  12.6 0.6 copy-start.7
  12.7 0.6 copy-start.8
  12.7 1.0 copy-start.3
  12.7 1.3 copy-start.4
  14.0 68.4 %all-to-all-start = ((bf16[16,128,1024]{2,1,0:T(8,128)(2,1)}), bf16[16,128,1024]{2,1,0:T(8,128)(2,1)}, u32[]{:S(2)}, u32[]{:S(2)}) async-start(bf16[16,128,1024]{2,1,0:T(8,128)(2,1)} %get-tuple-element.38), calls=%async_computation | async-start | bytes 8388608 | tf_op jit(solution)/shard_map/all_to_all | solution.py:342
  19.1 12.2 %collective-permute-start.7 = (bf16[1,2,256,128]{3,2,1,0:T(8,128)(2,1)S(1)}, bf16[1,2,256,128]{3,2,1,0:T(8,128)(2,1)S(1)}, u32[]{:S(2)}, u32[]{:S(2)}) collective-permute-start(bf16[1,2,256,128]{3,2,1,0:T(8,128)(2,1)S(1)} %fusion.5), channel_id=1, source_target_pairs={{0,12},{2,14},{4,8},{6,10},{8,4},{10,6},{12,0},{14,2},{1,13},{3,15... | collective-permute-start | bytes 393224 | tf_op jit(solution)/shard_map/ppermute | solution.py:330
  25.2 7.7 %collective-permute-start.6 = (bf16[1,2,256,128]{3,2,1,0:T(8,128)(2,1)S(1)}, bf16[1,2,256,128]{3,2,1,0:T(8,128)(2,1)S(1)}, u32[]{:S(2)}, u32[]{:S(2)}) collective-permute-start(bf16[1,2,256,128]{3,2,1,0:T(8,128)(2,1)S(1)} %fusion.5), channel_id=1, source_target_pairs={{0,4},{2,6},{4,0},{6,2},{8,12},{10,14},{12,8},{14,10},{1,5},{3,7},... | collective-permute-start | bytes 393224 | tf_op jit(solution)/shard_map/ppermute | solution.py:330
  26.4 12.2 %collective-permute-start.5 = (bf16[1,2,256,128]{3,2,1,0:T(8,128)(2,1)S(1)}, bf16[1,2,256,128]{3,2,1,0:T(8,128)(2,1)S(1)}, u32[]{:S(2)}, u32[]{:S(2)}) collective-permute-start(bf16[1,2,256,128]{3,2,1,0:T(8,128)(2,1)S(1)} %fusion.5), channel_id=1, source_target_pairs={{0,8},{2,10},{4,12},{6,14},{8,0},{10,2},{12,4},{14,6},{1,9},{3,11}... | collective-permute-start | bytes 393224 | tf_op jit(solution)/shard_map/ppermute | solution.py:330
  27.4 57.6 %collective-permute-start.11 = (bf16[4,768,256]{2,1,0:T(8,128)(2,1)}, bf16[4,768,256]{2,1,0:T(8,128)(2,1)}, u32[]{:S(2)}, u32[]{:S(2)}) collective-permute-start(bf16[4,768,256]{2,1,0:T(8,128)(2,1)} %get-tuple-element.54), channel_id=1, source_target_pairs={{0,1},{1,0},{2,3},{3,2},{4,5},{5,4},{6,7},{7,6},{8,9},{9,8},{10,11... | collective-permute-start | bytes 4718600 | tf_op jit(solution)/shard_map/ppermute | solution.py:327
  38.7 11.7 %collective-permute-start.8 = (bf16[4,2,256,128]{3,2,1,0:T(8,128)(2,1)S(1)}, bf16[4,2,256,128]{3,2,1,0:T(8,128)(2,1)S(1)}, u32[]{:S(2)}, u32[]{:S(2)}) collective-permute-start(bf16[4,2,256,128]{3,2,1,0:T(8,128)(2,1)S(1)} %pad_maximum_fusion), channel_id=1, source_target_pairs={{0,2},{2,0},{4,6},{6,4},{8,10},{10,8},{12,14},{14,12},{1,3},{3,1},... | collective-permute-start | bytes 1572872 | tf_op jit(solution)/shard_map/ppermute | solution.py:330
  50.4 0.8 copy-start.6
  65.5 11.1 %collective-permute-start.9 = (bf16[4,2,256,128]{3,2,1,0:T(8,128)(2,1)}, bf16[4,2,256,128]{3,2,1,0:T(8,128)(2,1)S(1)}, u32[]{:S(2)}, u32[]{:S(2)}) collective-permute-start(bf16[4,2,256,128]{3,2,1,0:T(8,128)(2,1)} %get-tuple-element.46), channel_id=1, source_target_pairs={{0,2},{2,0},{4,6},{6,4},{8,10},{10,8},{12,14},{14,12},{1,3},{3,1},... | collective-permute-start | bytes 1572872 | tf_op jit(solution)/shard_map/ppermute | solution.py:330
  67.4 9.3 %copy-start.1 = (f32[2,2,256,128]{3,2,1,0:T(8,128)S(1)}, f32[2,2,256,128]{3,2,1,0:T(8,128)}, u32[]{:S(2)}) copy-start(f32[2,2,256,128]{3,2,1,0:T(8,128)} %get-tuple-element.49) | copy-start | bytes 1572868
  83.7 3.6 %collective-permute-start.10 = (bf16[16,128,256]{2,1,0:T(8,128)(2,1)S(1)}, bf16[16,128,256]{2,1,0:T(8,128)(2,1)S(1)}, u32[]{:S(2)}, u32[]{:S(2)}) collective-permute-start(bf16[16,128,256]{2,1,0:T(8,128)(2,1)S(1)} %slice.38), channel_id=1, source_target_pairs={{0,1},{1,0},{2,3},{3,2},{4,5},{5,4},{6,7},{7,6},{8,9},{9,8},{10,11... | collective-permute-start | bytes 3145736 | tf_op jit(solution)/shard_map/ppermute | solution.py:327
  87.3 1.0 copy-start.5
  95.7 32.8 %collective-permute-start.16 = (bf16[4,768,256]{2,1,0:T(8,128)(2,1)}, bf16[4,768,256]{2,1,0:T(8,128)(2,1)S(1)}, u32[]{:S(2)}, u32[]{:S(2)}) collective-permute-start(bf16[4,768,256]{2,1,0:T(8,128)(2,1)} %get-tuple-element.62), channel_id=1, source_target_pairs={{0,1},{1,0},{2,3},{3,2},{4,5},{5,4},{6,7},{7,6},{8,9},{9,8},{10,11... | collective-permute-start | bytes 4718600 | tf_op jit(solution)/shard_map/ppermute | solution.py:327
  96.1 23.4 %collective-permute-start.12 = (bf16[2,256,128]{2,1,0:T(8,128)(2,1)S(1)}, bf16[2,256,128]{2,1,0:T(8,128)(2,1)S(1)}, u32[]{:S(2)}, u32[]{:S(2)}) collective-permute-start(bf16[2,256,128]{2,1,0:T(8,128)(2,1)S(1)} %fusion.6), channel_id=1, source_target_pairs={{0,8},{2,10},{4,12},{6,14},{8,0},{10,2},{12,4},{14,6},{1,9},{3,11}... | collective-permute-start | bytes 393224 | tf_op jit(solution)/shard_map/ppermute | solution.py:330
  104.7 21.3 %all-to-all-start.1 = ((f32[256,1,128]{2,1,0:T(1,128)}), f32[256,1,128]{2,1,0:T(1,128)S(1)}, u32[]{:S(2)}, u32[]{:S(2)}) async-start(f32[256,1,128]{2,1,0:T(1,128)} %bitcast.7), calls=%async_computation.1 | async-start | bytes 262144 | tf_op jit(solution)/shard_map/all_to_all | solution.py:367
  111.9 10.7 %collective-permute-start.14 = (bf16[2,256,128]{2,1,0:T(8,128)(2,1)S(1)}, bf16[2,256,128]{2,1,0:T(8,128)(2,1)S(1)}, u32[]{:S(2)}, u32[]{:S(2)}) collective-permute-start(bf16[2,256,128]{2,1,0:T(8,128)(2,1)S(1)} %get-tuple-element.74), channel_id=1, source_target_pairs={{0,12},{2,14},{4,8},{6,10},{8,4},{10,6},{12,0},{14,2},{1,13},{3,15... | collective-permute-start | bytes 393224 | tf_op jit(solution)/shard_map/ppermute | solution.py:330
  117.0 8.9 %collective-permute-start.13 = (bf16[2,256,128]{2,1,0:T(8,128)(2,1)S(1)}, bf16[2,256,128]{2,1,0:T(8,128)(2,1)S(1)}, u32[]{:S(2)}, u32[]{:S(2)}) collective-permute-start(bf16[2,256,128]{2,1,0:T(8,128)(2,1)S(1)} %get-tuple-element.75), channel_id=1, source_target_pairs={{0,4},{2,6},{4,0},{6,2},{8,12},{10,14},{12,8},{14,10},{1,5},{3,7},... | collective-permute-start | bytes 393224 | tf_op jit(solution)/shard_map/ppermute | solution.py:330
  118.5 8.3 %collective-permute-start.15 = (bf16[1,128,2048]{2,1,0:T(8,128)(2,1)}, bf16[1,128,2048]{2,1,0:T(8,128)(2,1)S(1)}, u32[]{:S(2)}, u32[]{:S(2)}) collective-permute-start(bf16[1,128,2048]{2,1,0:T(8,128)(2,1)} %bitcast.38), channel_id=1, source_target_pairs={{0,1},{1,0},{2,3},{3,2},{4,5},{5,4},{6,7},{7,6},{8,9},{9,8},{10,11... | collective-permute-start | bytes 1572872 | tf_op jit(solution)/shard_map/ppermute | solution.py:327
  125.9 3.8 %copy-start = (f32[256,1,128]{2,1,0:T(1,128)}, f32[256,1,128]{2,1,0:T(1,128)S(1)}, u32[]{:S(2)}) copy-start(f32[256,1,128]{2,1,0:T(1,128)S(1)} %all-to-all-done.1) | copy-start | bytes 393220
  126.0 1.8 %collective-permute-start.17 = (f32[2,128,128]{2,1,0:T(8,128)S(1)}, f32[2,128,128]{2,1,0:T(8,128)S(1)}, u32[]{:S(2)}, u32[]{:S(2)}) collective-permute-start(f32[2,128,128]{2,1,0:T(8,128)S(1)} %get-tuple-element.73), channel_id=1, source_target_pairs={{0,1},{1,0},{2,3},{3,2},{4,5},{5,4},{6,7},{7,6},{8,9},{9,8},{10,11... | collective-permute-start | bytes 393224 | tf_op jit(solution)/shard_map/ppermute | solution.py:327

commit v3 on v2

--- a/solution.py
+++ b/solution.py
@@ -340,25 +340,18 @@
     sent, sibs, own = lax.optimization_barrier((sent, sibs, own))
     rows = list(zip((queries, out_grad, log_norms, row_deltas), sibs))
     got = lax.all_to_all(sent, "prompt", 0, 0, tiled=True)
-    keys = [own] + [across(own, k) for k in (4, 2, 6)]
-    keys_a = jnp.concatenate(keys[:2], axis=0)
-    keys_c = jnp.concatenate(keys[2:], axis=0)
-    keys_b = across(jnp.concatenate([keys_a, keys_c], axis=0), 1)
+    near = [across(own, k) for k in (4, 2, 6)]
     w_sib = swap(w_give)
 
-    kv_a, dq = attend(core, rows, keys_a, F32)
-    kv_b, dq = attend(core, rows, keys_b, BF, dq)
-    kv_c, query_grad, query_sib = attend(core, rows, keys_c, F32, dq, last=True)
-    kv_b = across(kv_b, 1)
-    kv_a, kv_b, kv_c = lax.optimization_barrier((kv_a, kv_b, kv_c))
-    kv_b = kv_b.astype(F32)
-    kv_a, kv_c = kv_a + kv_b[:2], (kv_c + kv_b[2:]).astype(BF)
-    got, kv_a, kv_c, query_sib = lax.optimization_barrier((got, kv_a, kv_c, query_sib))
-    kv_parts = [
-        across(kv_a[1].astype(BF), 4),
-        across(kv_c[0], 2),
-        across(kv_c[1], 6),
-    ]
+    kv_own, dq = attend(core, rows, own, F32)
+    near, dq = lax.optimization_barrier((near, dq))
+    far = across(jnp.concatenate([own] + near, axis=0), 1)
+    kv_near, dq = attend(core, rows, jnp.concatenate(near, axis=0), F32, dq)
+    kv_far, query_grad, query_sib = attend(core, rows, far, BF, dq, last=True)
+    kv_far = across(kv_far, 1).astype(F32)
+    kv_low = (kv_near + kv_far[1:]).astype(BF)
+    kv_parts = [across(kv_low[i], k) for i, k in enumerate((4, 2, 6))]
+    got, kv_parts, query_sib = lax.optimization_barrier((got, kv_parts, query_sib))
     query_sib = swap(query_sib[None])
 
     dots, w_down_grad, w_part = experts(core, got, swap(got[:, :, HALF:]), w_down, w_sib)
@@ -366,8 +359,7 @@
     dots = jnp.broadcast_to(dots, (NP, 2 * NZ, SLOTS)).reshape(NP * 2 * NZ, SLOTS)
     dots = lax.all_to_all(dots, ("prompt", "z", "c"), 0, 0, tiled=True)
     w_part = swap(w_part)
-    dots, kv_parts = lax.optimization_barrier((dots, kv_parts))
-    kv_sum = kv_a[0]
+    kv_sum = kv_own[0] + kv_far[0]
     for part in kv_parts:
         kv_sum = kv_sum + part.astype(F32)
     query_grad = join(

time: 133 us -> 141 us (1.060)
  waiting for transfers between devices: 25.6 us -> 35.2 us
  starting transfers between devices: 44.5 us -> 42.8 us
    ppermute x8, starting transfers between devices: 23.5 us -> 16.4 us  [across(): return lax.ppermute(x, 'z', [(i, i ^ by) for i in range(NZ)])]
    all_to_all x1, waiting for transfers between devices: 0.01 us -> 6.82 us  [body(): dots = lax.all_to_all(dots, ('prompt', 'z', 'c'), 0, 0, tiled=True)]
    ppermute x8, waiting for transfers between devices: 18.5 us -> 25 us  [across(): return lax.ppermute(x, 'z', [(i, i ^ by) for i in range(NZ)])]
    all_to_all x1, waiting for transfers between devices: 4.62 us -> 0.01 us  [body(): got = lax.all_to_all(sent, 'prompt', 0, 0, tiled=True)]
    all_to_all x1, starting transfers between devices: 7.23 us -> 10 us  [body(): dots = lax.all_to_all(dots, ('prompt', 'z', 'c'), 0, 0, tiled=True)]
    ppermute x10, starting transfers between devices: 8.65 us -> 11.3 us  [swap(): return lax.ppermute(x, 'c', SWAP)]
    unnamed x18 -> x24, local copies, waits for them, and re-layouts: 3.09 us -> 2.77 us
  transfers between devices with their start and end apart: 20 -> 20, of which waited for: 10 -> 8; matrix products, arithmetic and copies ran while one was open for 5% -> 5% of each run, Pallas kernels for 31% -> 30%
where the time goes in v3:
time: 141 us; the launch traced here: 140 us
  Pallas kernels  52.1 us (37%)
  starting transfers between devices  42.8 us (30%)
  waiting for transfers between devices  35.2 us (25%)
  local copies, waits for them, and re-layouts  5.02 us (4%)
  other arithmetic  4.43 us (3%)
    pallas_call x3, Pallas kernels, attend(): pl.pallas_call(functools.partial(attend_kernel, first, last), out_shape=t...  32.4 us
    ppermute x8, waiting for transfers between devices, across(): return lax.ppermute(x, 'z', [(i, i ^ by) for i in range(NZ)])  25 us
    ppermute x8, starting transfers between devices, across(): return lax.ppermute(x, 'z', [(i, i ^ by) for i in range(NZ)])  16.4 us
    ppermute x10, starting transfers between devices, swap(): return lax.ppermute(x, 'c', SWAP)  11.3 us
    all_to_all x1, starting transfers between devices, body(): dots = lax.all_to_all(dots, ('prompt', 'z', 'c'), 0, 0, tiled=True)  10 us
    pallas_call x1, Pallas kernels, dispatch(): pl.pallas_call(dispatch_kernel, out_shape=(jax.ShapeDtypeStruct((NP, SLOT...  7.59 us
    pallas_call x1, Pallas kernels, experts(): pl.pallas_call(expert_kernel, out_shape=(jax.ShapeDtypeStruct((LOCAL, 1,...  7.4 us
    all_to_all x1, waiting for transfers between devices, body(): dots = lax.all_to_all(dots, ('prompt', 'z', 'c'), 0, 0, tiled=True)  6.82 us
  transfers between devices with their start and end apart: 20, of which 8 were waited for; matrix products, arithmetic and copies ran while one was open for 5% of the time, Pallas kernels for 30%

profile of v3, /device:TPU:1, one launch (start us, length us, event | category | flops | bytes accessed | tf_op | source)
XLA Modules:
  0.0 140.4 jit_solution(17392368835512420401)
XLA Ops:
  0.6 3.3 %collective-permute-start = (bf16[1,128,4096]{2,1,0:T(8,128)(2,1)}, bf16[1,128,4096]{2,1,0:T(8,128)(2,1)S(1)}, u32[]{:S(2)}, u32[]{:S(2)}) collective-permute-start(bf16[1,128,4096]{2,1,0:T(8,128)(2,1)} %refs_1_.5), channel_id=1, source_target_pairs={{0,1},{1,0},{2,3},{3,2},{4,5},{5,4},{6,7},{7,6},{8,9},{9,8},{10,11... | collective-permute-start | bytes 3145736 | tf_op jit(solution)/shard_map/ppermute | solution.py:327
  4.0 0.1 collective-permute-start.1
  4.1 0.4 collective-permute-start.2
  4.5 0.1 collective-permute-start.3
  4.6 0.4 collective-permute-start.4
  5.0 7.6 %dispatch.1 = (bf16[16,128,1024]{2,1,0:T(8,128)(2,1)}, s32[8,128]{1,0:T(8,128)}, bf16[4,768,256]{2,1,0:T(8,128)(2,1)}) custom-call(s32[1]{0:T(128)} %bitcast.c_ref.refs_0_, s32[8,128]{1,0:T(8,128)} %bitcast.41, f32[8,128]{1,0:T(8,128)} %bitcast.36, bf16[128,256]{1,0:T(8,128)(2,1)} %grad_ref.1, bf16[1024,1536]{1,0:T(8,128)(2,1)} %bitcast.39, ...), custom_call_target="tpu_custom_call" | custom-call | flops 3221225472 | bytes 6291456 | tf_op jit(solution)/shard_map/dispatch/pallas_call | solution.py:94
  12.6 0.0 collective-permute-done.4
  12.6 0.0 copy-start.2
  12.7 0.0 collective-permute-done.2.refs_6_
  12.7 0.0 collective-permute-done.3.refs_8_
  12.7 0.0 collective-permute-done.refs_2_
  12.7 0.0 collective-permute-done.1.refs_4_
  12.7 0.6 copy-done.10
  13.3 0.5 copy-done.7
  13.7 0.3 copy-done.8
  14.0 5.1 %all-to-all-start = ((bf16[16,128,1024]{2,1,0:T(8,128)(2,1)}), bf16[16,128,1024]{2,1,0:T(8,128)(2,1)}, u32[]{:S(2)}, u32[]{:S(2)}) async-start(bf16[16,128,1024]{2,1,0:T(8,128)(2,1)} %get-tuple-element.36), calls=%async_computation | async-start | bytes 8388608 | tf_op jit(solution)/shard_map/all_to_all | solution.py:342
  19.1 6.1 %collective-permute-start.7 = (bf16[1,2,256,128]{3,2,1,0:T(8,128)(2,1)S(1)}, bf16[1,2,256,128]{3,2,1,0:T(8,128)(2,1)S(1)}, u32[]{:S(2)}, u32[]{:S(2)}) collective-permute-start(bf16[1,2,256,128]{3,2,1,0:T(8,128)(2,1)S(1)} %fusion.7.refs_9_), channel_id=1, source_target_pairs={{0,12},{2,14},{4,8},{6,10},{8,4},{10,6},{12,0},{14,2},{1,13},{3,15... | collective-permute-start | bytes 393224 | tf_op jit(solution)/shard_map/ppermute | solution.py:330
  25.2 1.2 collective-permute-start.6
  26.4 1.0 collective-permute-start.5
  27.4 6.4 %attend_1.1 = (f32[1,2,256,128]{3,2,1,0:T(8,128)}, f32[256,2048]{1,0:T(8,128)}) custom-call(s32[1]{0:T(128)} %bitcast.c_ref.refs_0_, bf16[1,128,4096]{2,1,0:T(8,128)(2,1)} %refs_1_.5, bf16[1,128,4096]{2,1,0:T(8,128)(2,1)} %copy-done.7, bf16[1,128,4096]{2,1,0:T(8,128)(2,1)} %refs_3_.5, bf16[1,128,4096]{2,1,0:T(8,128)(2,1)} %copy-done.8, ...), custom_call_target="tpu_custom_call" | custom-call | flops 2684354560 | bytes 8388608 | tf_op jit(solution)/shard_map/attend_1/pallas_call | solution.py:269
  33.8 0.0 collective-permute-done.7
  33.8 0.0 collective-permute-done.6
  33.8 4.8 %collective-permute-done.5 = bf16[1,2,256,128]{3,2,1,0:T(8,128)(2,1)S(1)} collective-permute-done((bf16[1,2,256,128]{3,2,1,0:T(8,128)(2,1)S(1)}, bf16[1,2,256,128]{3,2,1,0:T(8,128)(2,1)S(1)}, u32[]{:S(2)}, u32[]{:S(2)}) %collective-permute-start.5) | collective-permute-done | bytes 131104 | tf_op jit(solution)/shard_map/ppermute | solution.py:330
  38.6 1.0 pad_maximum_fusion
  39.6 0.7 collective-permute-start.8
  40.3 0.8 pad_maximum_fusion.1.refs_9_
  41.1 11.8 %attend_3.1 = (f32[3,2,256,128]{3,2,1,0:T(8,128)}, f32[256,2048]{1,0:T(8,128)}) custom-call(s32[1]{0:T(128)} %bitcast.c_ref.refs_0_, bf16[1,128,4096]{2,1,0:T(8,128)(2,1)} %refs_1_.5, bf16[1,128,4096]{2,1,0:T(8,128)(2,1)} %copy-done.7, bf16[1,128,4096]{2,1,0:T(8,128)(2,1)} %refs_3_.5, bf16[1,128,4096]{2,1,0:T(8,128)(2,1)} %copy-done.8, ...), custom_call_target="tpu_custom_call" | custom-call | flops 8053063680 | bytes 8388608 | tf_op jit(solution)/shard_map/attend_3/pallas_call | solution.py:269
  52.8 0.0 collective-permute-done.8.refs_9_
  52.8 0.0 copy-start.9
  52.9 0.8 copy-done.9
  53.6 14.3 %attend_4.1 = (bf16[4,2,256,128]{3,2,1,0:T(8,128)(2,1)}, bf16[1,128,4096]{2,1,0:T(8,128)(2,1)}, bf16[128,2048]{1,0:T(8,128)(2,1)}) custom-call(s32[1]{0:T(128)} %bitcast.c_ref.refs_0_, bf16[1,128,4096]{2,1,0:T(8,128)(2,1)} %refs_1_.5, bf16[1,128,4096]{2,1,0:T(8,128)(2,1)} %copy-done.7, bf16[1,128,4096]{2,1,0:T(8,128)(2,1)} %refs_3_.5, ...), custom_call_target="tpu_custom_call" | custom-call | flops 10737418240 | bytes 8388608 | tf_op jit(solution)/shard_map/attend_4/pallas_call | solution.py:269
  68.0 1.1 collective-permute-start.9
  69.1 2.4 %collective-permute-start.14 = (bf16[4,768,256]{2,1,0:T(8,128)(2,1)}, bf16[4,768,256]{2,1,0:T(8,128)(2,1)}, u32[]{:S(2)}, u32[]{:S(2)}) collective-permute-start(bf16[4,768,256]{2,1,0:T(8,128)(2,1)} %get-tuple-element.52), channel_id=1, source_target_pairs={{0,1},{1,0},{2,3},{3,2},{4,5},{5,4},{6,7},{7,6},{8,9},{9,8},{10,11... | collective-permute-start | bytes 4718600 | tf_op jit(solution)/shard_map/ppermute | solution.py:327
  71.5 8.8 %collective-permute-done.9 = bf16[4,2,256,128]{3,2,1,0:T(8,128)(2,1)S(1)} collective-permute-done((bf16[4,2,256,128]{3,2,1,0:T(8,128)(2,1)}, bf16[4,2,256,128]{3,2,1,0:T(8,128)(2,1)S(1)}, u32[]{:S(2)}, u32[]{:S(2)}) %collective-permute-start.9) | collective-permute-done | bytes 524320 | tf_op jit(solution)/shard_map/ppermute | solution.py:330
  80.3 0.1 convert_element_type.15
  80.4 0.1 fusion
  80.5 4.1 %collective-permute-start.12 = (bf16[2,256,128]{2,1,0:T(8,128)(2,1)S(1)}, bf16[2,256,128]{2,1,0:T(8,128)(2,1)S(1)}, u32[]{:S(2)}, u32[]{:S(2)}) collective-permute-start(bf16[2,256,128]{2,1,0:T(8,128)(2,1)S(1)} %get-tuple-element.66), channel_id=1, source_target_pairs={{0,12},{2,14},{4,8},{6,10},{8,4},{10,6},{12,0},{14,2},{1,13},{3,15... | collective-permute-start | bytes 393224 | tf_op jit(solution)/shard_map/ppermute | solution.py:330
  84.6 0.0 collective-permute-start.11
  84.6 2.2 %collective-permute-start.10 = (bf16[2,256,128]{2,1,0:T(8,128)(2,1)S(1)}, bf16[2,256,128]{2,1,0:T(8,128)(2,1)S(1)}, u32[]{:S(2)}, u32[]{:S(2)}) collective-permute-start(bf16[2,256,128]{2,1,0:T(8,128)(2,1)S(1)} %get-tuple-element.68), channel_id=1, source_target_pairs={{0,8},{2,10},{4,12},{6,14},{8,0},{10,2},{12,4},{14,6},{1,9},{3,11}... | collective-permute-start | bytes 393224 | tf_op jit(solution)/shard_map/ppermute | solution.py:330
  86.8 0.3 collective-permute-done.12
  87.1 5.2 %collective-permute-done.11 = bf16[2,256,128]{2,1,0:T(8,128)(2,1)S(1)} collective-permute-done((bf16[2,256,128]{2,1,0:T(8,128)(2,1)S(1)}, bf16[2,256,128]{2,1,0:T(8,128)(2,1)S(1)}, u32[]{:S(2)}, u32[]{:S(2)}) %collective-permute-start.11) | collective-permute-done | bytes 131104 | tf_op jit(solution)/shard_map/ppermute | solution.py:330
  92.3 5.9 %collective-permute-done.10 = bf16[2,256,128]{2,1,0:T(8,128)(2,1)S(1)} collective-permute-done((bf16[2,256,128]{2,1,0:T(8,128)(2,1)S(1)}, bf16[2,256,128]{2,1,0:T(8,128)(2,1)S(1)}, u32[]{:S(2)}, u32[]{:S(2)}) %collective-permute-start.10) | collective-permute-done | bytes 131104 | tf_op jit(solution)/shard_map/ppermute | solution.py:330
  98.2 1.4 slice.36
  99.5 0.0 copy-start.3
  99.5 1.7 %collective-permute-start.13 = (bf16[16,128,256]{2,1,0:T(8,128)(2,1)S(1)}, bf16[16,128,256]{2,1,0:T(8,128)(2,1)}, u32[]{:S(2)}, u32[]{:S(2)}) collective-permute-start(bf16[16,128,256]{2,1,0:T(8,128)(2,1)S(1)} %slice.36), channel_id=1, source_target_pairs={{0,1},{1,0},{2,3},{3,2},{4,5},{5,4},{6,7},{7,6},{8,9},{9,8},{10,11... | collective-permute-start | bytes 3145736 | tf_op jit(solution)/shard_map/ppermute | solution.py:327
  101.3 0.0 collective-permute-done.14.wsib_ref
  101.3 2.4 %collective-permute-done.13.ssib_ref = bf16[16,128,256]{2,1,0:T(8,128)(2,1)} collective-permute-done((bf16[16,128,256]{2,1,0:T(8,128)(2,1)S(1)}, bf16[16,128,256]{2,1,0:T(8,128)(2,1)}, u32[]{:S(2)}, u32[]{:S(2)}) %collective-permute-start.13) | collective-permute-done | bytes 1048608 | tf_op jit(solution)/shard_map/ppermute | solution.py:327
  103.7 7.4 %experts.1 = (f32[4,1,512]{2,1,0:T(1,128)}, bf16[4,1536,256]{2,1,0:T(8,128)(2,1)}, bf16[4,768,256]{2,1,0:T(8,128)(2,1)}) custom-call(s32[1]{0:T(128)} %bitcast.c_ref.refs_0_, bf16[16,128,1024]{2,1,0:T(8,128)(2,1)} %all-to-all-done.got_ref, bf16[16,128,256]{2,1,0:T(8,128)(2,1)} %collective-permute-done.13.ssib_ref, bf16[4,1536,256]{2,1,0:T(8,128)(2,1)} %wown_ref.1, ...), custom_call_target="tpu_custom_call" | custom-call | flops 3221225472 | bytes 13631488 | tf_op jit(solution)/shard_map/experts/pallas_call | solution.py:140
  111.1 0.5 collective-permute-start.16
  111.6 0.1 collective-permute-start.15
  111.7 1.0 fusion.4
  112.7 0.7 reduce
  113.5 0.1 reshape.77
  113.6 0.1 broadcast_in_dim.19
  113.6 0.7 broadcast_in_dim.20
  114.3 10.0 %all-to-all-start.1 = ((f32[256,1,128]{2,1,0:T(1,128)}), f32[256,1,128]{2,1,0:T(1,128)S(1)}, u32[]{:S(2)}, u32[]{:S(2)}) async-start(f32[256,1,128]{2,1,0:T(1,128)} %bitcast.10), calls=%async_computation.1 | async-start | bytes 262144 | tf_op jit(solution)/shard_map/all_to_all | solution.py:360
  124.4 2.2 %collective-permute-start.17 = (f32[2,128,128]{2,1,0:T(8,128)S(1)}, f32[2,128,128]{2,1,0:T(8,128)S(1)}, u32[]{:S(2)}, u32[]{:S(2)}) collective-permute-start(f32[2,128,128]{2,1,0:T(8,128)S(1)} %get-tuple-element.70), channel_id=1, source_target_pairs={{0,1},{1,0},{2,3},{3,2},{4,5},{5,4},{6,7},{7,6},{8,9},{9,8},{10,11... | collective-permute-start | bytes 393224 | tf_op jit(solution)/shard_map/ppermute | solution.py:327
  126.6 1.0 collective-permute-done.17
  127.6 0.7 maximum_select_fusion
  128.3 0.9 join_query.1
  129.2 1.2 join_down.1
  130.4 6.8 %all-to-all-done.1 = f32[256,1,128]{2,1,0:T(1,128)S(1)} async-done(((f32[256,1,128]{2,1,0:T(1,128)}), f32[256,1,128]{2,1,0:T(1,128)S(1)}, u32[]{:S(2)}, u32[]{:S(2)}) %all-to-all-start.1) | async-done | bytes 131104 | tf_op jit(solution)/shard_map/all_to_all | solution.py:360
  137.2 0.6 copy-done.1
  137.8 2.6 %collect.1 = f32[8,128]{1,0:T(8,128)} custom-call(s32[8,128]{1,0:T(8,128)} %get-tuple-element.64.slot_ref, f32[8,128]{1,0:T(8,128)} %bitcast.37, f32[256,128]{1,0:T(8,128)} %bitcast.31), custom_call_target="tpu_custom_call" | custom-call | flops 8388608 | bytes 262144 | tf_op jit(solution)/shard_map/collect/pallas_call | solution.py:301
  (23 shorter events, 0.1 us)
Async XLA Ops:
  0.6 12.1 %collective-permute-start = (bf16[1,128,4096]{2,1,0:T(8,128)(2,1)}, bf16[1,128,4096]{2,1,0:T(8,128)(2,1)S(1)}, u32[]{:S(2)}, u32[]{:S(2)}) collective-permute-start(bf16[1,128,4096]{2,1,0:T(8,128)(2,1)} %refs_1_.5), channel_id=1, source_target_pairs={{0,1},{1,0},{2,3},{3,2},{4,5},{5,4},{6,7},{7,6},{8,9},{9,8},{10,11... | collective-permute-start | bytes 3145736 | tf_op jit(solution)/shard_map/ppermute | solution.py:327
  4.0 8.8 %collective-permute-start.1 = (bf16[1,128,4096]{2,1,0:T(8,128)(2,1)}, bf16[1,128,4096]{2,1,0:T(8,128)(2,1)S(1)}, u32[]{:S(2)}, u32[]{:S(2)}) collective-permute-start(bf16[1,128,4096]{2,1,0:T(8,128)(2,1)} %refs_3_.5), channel_id=1, source_target_pairs={{0,1},{1,0},{2,3},{3,2},{4,5},{5,4},{6,7},{7,6},{8,9},{9,8},{10,11... | collective-permute-start | bytes 3145736 | tf_op jit(solution)/shard_map/ppermute | solution.py:327
  4.1 8.6 %collective-permute-start.2 = (f32[1,32,128]{2,1,0:T(8,128)}, f32[1,32,128]{2,1,0:T(8,128)S(1)}, u32[]{:S(2)}, u32[]{:S(2)}) collective-permute-start(f32[1,32,128]{2,1,0:T(8,128)} %refs_5_.5), channel_id=1, source_target_pairs={{0,1},{1,0},{2,3},{3,2},{4,5},{5,4},{6,7},{7,6},{8,9},{9,8},{10,11... | collective-permute-start | bytes 49160 | tf_op jit(solution)/shard_map/ppermute | solution.py:327
  4.5 8.2 %collective-permute-start.3 = (f32[1,32,128]{2,1,0:T(8,128)}, f32[1,32,128]{2,1,0:T(8,128)S(1)}, u32[]{:S(2)}, u32[]{:S(2)}) collective-permute-start(f32[1,32,128]{2,1,0:T(8,128)} %refs_7_.5), channel_id=1, source_target_pairs={{0,1},{1,0},{2,3},{3,2},{4,5},{5,4},{6,7},{7,6},{8,9},{9,8},{10,11... | collective-permute-start | bytes 49160 | tf_op jit(solution)/shard_map/ppermute | solution.py:327
  4.6 8.0 %collective-permute-start.4 = (bf16[2,128,256]{2,1,0:T(8,128)(2,1)}, bf16[2,128,256]{2,1,0:T(8,128)(2,1)S(1)}, u32[]{:S(2)}, u32[]{:S(2)}) collective-permute-start(bf16[2,128,256]{2,1,0:T(8,128)(2,1)} %bitcast.34), channel_id=1, source_target_pairs={{0,1},{1,0},{2,3},{3,2},{4,5},{5,4},{6,7},{7,6},{8,9},{9,8},{10,11... | collective-permute-start | bytes 393224 | tf_op jit(solution)/shard_map/ppermute | solution.py:327
  5.0 7.6 %copy-start.6 = (bf16[1,2,128,256]{3,2,1,0:T(8,128)(2,1)S(1)}, bf16[1,2,128,256]{3,2,1,0:T(8,128)(2,1)}, u32[]{:S(2)}) copy-start(bf16[1,2,128,256]{3,2,1,0:T(8,128)(2,1)} %param.14) | copy-start | bytes 393220
  12.6 14.8 %copy-start.2 = (bf16[1,2,256,128]{3,2,1,0:T(8,128)(2,1)}, bf16[1,2,256,128]{3,2,1,0:T(8,128)(2,1)S(1)}, u32[]{:S(2)}) copy-start(bf16[1,2,256,128]{3,2,1,0:T(8,128)(2,1)S(1)} %fusion.7.refs_9_) | copy-start | bytes 393220
  12.7 0.6 copy-start.10
  12.7 0.6 copy-start.11
  12.7 1.0 copy-start.7
  12.7 1.3 copy-start.8
  14.0 84.1 %all-to-all-start = ((bf16[16,128,1024]{2,1,0:T(8,128)(2,1)}), bf16[16,128,1024]{2,1,0:T(8,128)(2,1)}, u32[]{:S(2)}, u32[]{:S(2)}) async-start(bf16[16,128,1024]{2,1,0:T(8,128)(2,1)} %get-tuple-element.36), calls=%async_computation | async-start | bytes 8388608 | tf_op jit(solution)/shard_map/all_to_all | solution.py:342
  19.1 14.7 %collective-permute-start.7 = (bf16[1,2,256,128]{3,2,1,0:T(8,128)(2,1)S(1)}, bf16[1,2,256,128]{3,2,1,0:T(8,128)(2,1)S(1)}, u32[]{:S(2)}, u32[]{:S(2)}) collective-permute-start(bf16[1,2,256,128]{3,2,1,0:T(8,128)(2,1)S(1)} %fusion.7.refs_9_), channel_id=1, source_target_pairs={{0,12},{2,14},{4,8},{6,10},{8,4},{10,6},{12,0},{14,2},{1,13},{3,15... | collective-permute-start | bytes 393224 | tf_op jit(solution)/shard_map/ppermute | solution.py:330
  25.2 8.6 %collective-permute-start.6 = (bf16[1,2,256,128]{3,2,1,0:T(8,128)(2,1)S(1)}, bf16[1,2,256,128]{3,2,1,0:T(8,128)(2,1)S(1)}, u32[]{:S(2)}, u32[]{:S(2)}) collective-permute-start(bf16[1,2,256,128]{3,2,1,0:T(8,128)(2,1)S(1)} %fusion.7.refs_9_), channel_id=1, source_target_pairs={{0,4},{2,6},{4,0},{6,2},{8,12},{10,14},{12,8},{14,10},{1,5},{3,7},... | collective-permute-start | bytes 393224 | tf_op jit(solution)/shard_map/ppermute | solution.py:330
  26.4 12.2 %collective-permute-start.5 = (bf16[1,2,256,128]{3,2,1,0:T(8,128)(2,1)S(1)}, bf16[1,2,256,128]{3,2,1,0:T(8,128)(2,1)S(1)}, u32[]{:S(2)}, u32[]{:S(2)}) collective-permute-start(bf16[1,2,256,128]{3,2,1,0:T(8,128)(2,1)S(1)} %fusion.7.refs_9_), channel_id=1, source_target_pairs={{0,8},{2,10},{4,12},{6,14},{8,0},{10,2},{12,4},{14,6},{1,9},{3,11}... | collective-permute-start | bytes 393224 | tf_op jit(solution)/shard_map/ppermute | solution.py:330
  39.6 13.2 %collective-permute-start.8 = (bf16[4,2,256,128]{3,2,1,0:T(8,128)(2,1)S(1)}, bf16[4,2,256,128]{3,2,1,0:T(8,128)(2,1)S(1)}, u32[]{:S(2)}, u32[]{:S(2)}) collective-permute-start(bf16[4,2,256,128]{3,2,1,0:T(8,128)(2,1)S(1)} %pad_maximum_fusion), channel_id=1, source_target_pairs={{0,2},{2,0},{4,6},{6,4},{8,10},{10,8},{12,14},{14,12},{1,3},{3,1},... | collective-permute-start | bytes 1572872 | tf_op jit(solution)/shard_map/ppermute | solution.py:330
  52.8 0.8 copy-start.9
  53.6 26.7 %copy-start = (f32[3,2,256,128]{3,2,1,0:T(8,128)S(1)}, f32[3,2,256,128]{3,2,1,0:T(8,128)}, u32[]{:S(2)}) copy-start(f32[3,2,256,128]{3,2,1,0:T(8,128)} %get-tuple-element.47) | copy-start | bytes 2359300
  68.0 12.3 %collective-permute-start.9 = (bf16[4,2,256,128]{3,2,1,0:T(8,128)(2,1)}, bf16[4,2,256,128]{3,2,1,0:T(8,128)(2,1)S(1)}, u32[]{:S(2)}, u32[]{:S(2)}) collective-permute-start(bf16[4,2,256,128]{3,2,1,0:T(8,128)(2,1)} %get-tuple-element.49), channel_id=1, source_target_pairs={{0,2},{2,0},{4,6},{6,4},{8,10},{10,8},{12,14},{14,12},{1,3},{3,1},... | collective-permute-start | bytes 1572872 | tf_op jit(solution)/shard_map/ppermute | solution.py:330
  69.1 32.2 %collective-permute-start.14 = (bf16[4,768,256]{2,1,0:T(8,128)(2,1)}, bf16[4,768,256]{2,1,0:T(8,128)(2,1)}, u32[]{:S(2)}, u32[]{:S(2)}) collective-permute-start(bf16[4,768,256]{2,1,0:T(8,128)(2,1)} %get-tuple-element.52), channel_id=1, source_target_pairs={{0,1},{1,0},{2,3},{3,2},{4,5},{5,4},{6,7},{7,6},{8,9},{9,8},{10,11... | collective-permute-start | bytes 4718600 | tf_op jit(solution)/shard_map/ppermute | solution.py:327
  80.5 6.6 %collective-permute-start.12 = (bf16[2,256,128]{2,1,0:T(8,128)(2,1)S(1)}, bf16[2,256,128]{2,1,0:T(8,128)(2,1)S(1)}, u32[]{:S(2)}, u32[]{:S(2)}) collective-permute-start(bf16[2,256,128]{2,1,0:T(8,128)(2,1)S(1)} %get-tuple-element.66), channel_id=1, source_target_pairs={{0,12},{2,14},{4,8},{6,10},{8,4},{10,6},{12,0},{14,2},{1,13},{3,15... | collective-permute-start | bytes 393224 | tf_op jit(solution)/shard_map/ppermute | solution.py:330
  84.6 7.7 %collective-permute-start.11 = (bf16[2,256,128]{2,1,0:T(8,128)(2,1)S(1)}, bf16[2,256,128]{2,1,0:T(8,128)(2,1)S(1)}, u32[]{:S(2)}, u32[]{:S(2)}) collective-permute-start(bf16[2,256,128]{2,1,0:T(8,128)(2,1)S(1)} %get-tuple-element.67), channel_id=1, source_target_pairs={{0,4},{2,6},{4,0},{6,2},{8,12},{10,14},{12,8},{14,10},{1,5},{3,7},... | collective-permute-start | bytes 393224 | tf_op jit(solution)/shard_map/ppermute | solution.py:330
  84.6 13.6 %collective-permute-start.10 = (bf16[2,256,128]{2,1,0:T(8,128)(2,1)S(1)}, bf16[2,256,128]{2,1,0:T(8,128)(2,1)S(1)}, u32[]{:S(2)}, u32[]{:S(2)}) collective-permute-start(bf16[2,256,128]{2,1,0:T(8,128)(2,1)S(1)} %get-tuple-element.68), channel_id=1, source_target_pairs={{0,8},{2,10},{4,12},{6,14},{8,0},{10,2},{12,4},{14,6},{1,9},{3,11}... | collective-permute-start | bytes 393224 | tf_op jit(solution)/shard_map/ppermute | solution.py:330
  92.3 18.8 %copy-start.4 = (bf16[2,256,128]{2,1,0:T(8,128)(2,1)}, bf16[2,256,128]{2,1,0:T(8,128)(2,1)S(1)}, u32[]{:S(2)}) copy-start(bf16[2,256,128]{2,1,0:T(8,128)(2,1)S(1)} %collective-permute-done.11) | copy-start | bytes 393220
  98.2 12.9 %copy-start.5 = (bf16[2,256,128]{2,1,0:T(8,128)(2,1)}, bf16[2,256,128]{2,1,0:T(8,128)(2,1)S(1)}, u32[]{:S(2)}) copy-start(bf16[2,256,128]{2,1,0:T(8,128)(2,1)S(1)} %collective-permute-done.10) | copy-start | bytes 393220
  99.5 12.2 %copy-start.3 = (f32[1,2,256,128]{3,2,1,0:T(8,128)S(1)}, f32[1,2,256,128]{3,2,1,0:T(8,128)}, u32[]{:S(2)}) copy-start(f32[1,2,256,128]{3,2,1,0:T(8,128)} %get-tuple-element.59) | copy-start | bytes 786436
  99.5 4.1 %collective-permute-start.13 = (bf16[16,128,256]{2,1,0:T(8,128)(2,1)S(1)}, bf16[16,128,256]{2,1,0:T(8,128)(2,1)}, u32[]{:S(2)}, u32[]{:S(2)}) collective-permute-start(bf16[16,128,256]{2,1,0:T(8,128)(2,1)S(1)} %slice.36), channel_id=1, source_target_pairs={{0,1},{1,0},{2,3},{3,2},{4,5},{5,4},{6,7},{7,6},{8,9},{9,8},{10,11... | collective-permute-start | bytes 3145736 | tf_op jit(solution)/shard_map/ppermute | solution.py:327
  111.1 18.1 %collective-permute-start.16 = (bf16[4,768,256]{2,1,0:T(8,128)(2,1)}, bf16[4,768,256]{2,1,0:T(8,128)(2,1)S(1)}, u32[]{:S(2)}, u32[]{:S(2)}) collective-permute-start(bf16[4,768,256]{2,1,0:T(8,128)(2,1)} %get-tuple-element.57), channel_id=1, source_target_pairs={{0,1},{1,0},{2,3},{3,2},{4,5},{5,4},{6,7},{7,6},{8,9},{9,8},{10,11... | collective-permute-start | bytes 4718600 | tf_op jit(solution)/shard_map/ppermute | solution.py:327
  111.6 16.7 %collective-permute-start.15 = (bf16[1,128,2048]{2,1,0:T(8,128)(2,1)}, bf16[1,128,2048]{2,1,0:T(8,128)(2,1)S(1)}, u32[]{:S(2)}, u32[]{:S(2)}) collective-permute-start(bf16[1,128,2048]{2,1,0:T(8,128)(2,1)} %bitcast.40), channel_id=1, source_target_pairs={{0,1},{1,0},{2,3},{3,2},{4,5},{5,4},{6,7},{7,6},{8,9},{9,8},{10,11... | collective-permute-start | bytes 1572872 | tf_op jit(solution)/shard_map/ppermute | solution.py:327
  114.3 22.9 %all-to-all-start.1 = ((f32[256,1,128]{2,1,0:T(1,128)}), f32[256,1,128]{2,1,0:T(1,128)S(1)}, u32[]{:S(2)}, u32[]{:S(2)}) async-start(f32[256,1,128]{2,1,0:T(1,128)} %bitcast.10), calls=%async_computation.1 | async-start | bytes 262144 | tf_op jit(solution)/shard_map/all_to_all | solution.py:360
  124.4 3.2 %collective-permute-start.17 = (f32[2,128,128]{2,1,0:T(8,128)S(1)}, f32[2,128,128]{2,1,0:T(8,128)S(1)}, u32[]{:S(2)}, u32[]{:S(2)}) collective-permute-start(f32[2,128,128]{2,1,0:T(8,128)S(1)} %get-tuple-element.70), channel_id=1, source_target_pairs={{0,1},{1,0},{2,3},{3,2},{4,5},{5,4},{6,7},{7,6},{8,9},{9,8},{10,11... | collective-permute-start | bytes 393224 | tf_op jit(solution)/shard_map/ppermute | solution.py:327
  137.2 0.6 copy-start.1

commit v4 on v3

--- a/solution.py
+++ b/solution.py
@@ -350,8 +350,8 @@
     kv_far, query_grad, query_sib = attend(core, rows, far, BF, dq, last=True)
     kv_far = across(kv_far, 1).astype(F32)
     kv_low = (kv_near + kv_far[1:]).astype(BF)
+    got, kv_low, query_sib = lax.optimization_barrier((got, kv_low, query_sib))
     kv_parts = [across(kv_low[i], k) for i, k in enumerate((4, 2, 6))]
-    got, kv_parts, query_sib = lax.optimization_barrier((got, kv_parts, query_sib))
     query_sib = swap(query_sib[None])
 
     dots, w_down_grad, w_part = experts(core, got, swap(got[:, :, HALF:]), w_down, w_sib)
@@ -359,6 +359,7 @@
     dots = jnp.broadcast_to(dots, (NP, 2 * NZ, SLOTS)).reshape(NP * 2 * NZ, SLOTS)
     dots = lax.all_to_all(dots, ("prompt", "z", "c"), 0, 0, tiled=True)
     w_part = swap(w_part)
+    dots, kv_parts = lax.optimization_barrier((dots, kv_parts))
     kv_sum = kv_own[0] + kv_far[0]
     for part in kv_parts:
         kv_sum = kv_sum + part.astype(F32)

time: 141 us -> 137 us (0.972)
  waiting for transfers between devices: 35.2 us -> 26.1 us
  starting transfers between devices: 42.8 us -> 47.1 us
    all_to_all x1, waiting for transfers between devices: 6.82 us -> 0.01 us  [body(): dots = lax.all_to_all(dots, ('prompt', 'z', 'c'), 0, 0, tiled=True)]
    ppermute x8, waiting for transfers between devices: 25 us -> 21.7 us  [across(): return lax.ppermute(x, 'z', [(i, i ^ by) for i in range(NZ)])]
    all_to_all x1, starting transfers between devices: 10 us -> 12.2 us  [body(): dots = lax.all_to_all(dots, ('prompt', 'z', 'c'), 0, 0, tiled=True)]
    all_to_all x1, waiting for transfers between devices: 0.01 us -> 1.97 us  [body(): got = lax.all_to_all(sent, 'prompt', 0, 0, tiled=True)]
    unnamed x24 -> x26, local copies, waits for them, and re-layouts: 2.77 us -> 3.77 us
where the time goes in v4:
time: 137 us
  Pallas kernels  52.1 us (38%)
  starting transfers between devices  47.1 us (34%)
  waiting for transfers between devices  26.1 us (19%)
  local copies, waits for them, and re-layouts  5.95 us (4%)
  other arithmetic  4.54 us (3%)
    pallas_call x3, Pallas kernels, attend(): pl.pallas_call(functools.partial(attend_kernel, first, last), out_shape=t...  32.5 us
    ppermute x8, waiting for transfers between devices, across(): return lax.ppermute(x, 'z', [(i, i ^ by) for i in range(NZ)])  21.7 us
    ppermute x8, starting transfers between devices, across(): return lax.ppermute(x, 'z', [(i, i ^ by) for i in range(NZ)])  17.3 us
    ppermute x10, starting transfers between devices, swap(): return lax.ppermute(x, 'c', SWAP)  12.5 us
    all_to_all x1, starting transfers between devices, body(): dots = lax.all_to_all(dots, ('prompt', 'z', 'c'), 0, 0, tiled=True)  12.2 us
    pallas_call x1, Pallas kernels, dispatch(): pl.pallas_call(dispatch_kernel, out_shape=(jax.ShapeDtypeStruct((NP, SLOT...  7.61 us
    pallas_call x1, Pallas kernels, experts(): pl.pallas_call(expert_kernel, out_shape=(jax.ShapeDtypeStruct((LOCAL, 1,...  7.39 us
    all_to_all x1, starting transfers between devices, body(): got = lax.all_to_all(sent, 'prompt', 0, 0, tiled=True)  5.09 us
  transfers between devices with their start and end apart: 20, of which 8 were waited for; matrix products, arithmetic and copies ran while one was open for 5% of the time, Pallas kernels for 30%

profile of v4, /device:TPU:1, one launch (start us, length us, event | category | flops | bytes accessed | tf_op | source)
XLA Modules:
  0.0 136.7 jit_solution(4337673414686941176)
XLA Ops:
  0.6 3.3 %collective-permute-start = (bf16[1,128,4096]{2,1,0:T(8,128)(2,1)}, bf16[1,128,4096]{2,1,0:T(8,128)(2,1)S(1)}, u32[]{:S(2)}, u32[]{:S(2)}) collective-permute-start(bf16[1,128,4096]{2,1,0:T(8,128)(2,1)} %refs_1_.5), channel_id=1, source_target_pairs={{0,1},{1,0},{2,3},{3,2},{4,5},{5,4},{6,7},{7,6},{8,9},{9,8},{10,11... | collective-permute-start | bytes 3145736 | tf_op jit(solution)/shard_map/ppermute | solution.py:327
  4.0 0.1 collective-permute-start.1
  4.1 0.4 collective-permute-start.2
  4.5 0.1 collective-permute-start.3
  4.6 0.4 collective-permute-start.4
  5.0 7.6 %dispatch.1 = (bf16[16,128,1024]{2,1,0:T(8,128)(2,1)}, s32[8,128]{1,0:T(8,128)}, bf16[4,768,256]{2,1,0:T(8,128)(2,1)}) custom-call(s32[1]{0:T(128)} %bitcast.c_ref.refs_0_, s32[8,128]{1,0:T(8,128)} %bitcast.41, f32[8,128]{1,0:T(8,128)} %bitcast.36, bf16[128,256]{1,0:T(8,128)(2,1)} %grad_ref.1, bf16[1024,1536]{1,0:T(8,128)(2,1)} %bitcast.39, ...), custom_call_target="tpu_custom_call" | custom-call | flops 3221225472 | bytes 6291456 | tf_op jit(solution)/shard_map/dispatch/pallas_call | solution.py:94
  12.6 0.0 collective-permute-done.4
  12.7 0.0 copy-start.2
  12.7 0.0 collective-permute-done.2.refs_6_
  12.7 0.0 collective-permute-done.refs_2_
  12.7 0.0 collective-permute-done.1.refs_4_
  12.7 0.6 copy-done.11
  13.3 0.4 copy-done.7
  13.8 0.3 copy-done.8
  14.1 5.1 %all-to-all-start = ((bf16[16,128,1024]{2,1,0:T(8,128)(2,1)}), bf16[16,128,1024]{2,1,0:T(8,128)(2,1)}, u32[]{:S(2)}, u32[]{:S(2)}) async-start(bf16[16,128,1024]{2,1,0:T(8,128)(2,1)} %get-tuple-element.38), calls=%async_computation | async-start | bytes 8388608 | tf_op jit(solution)/shard_map/all_to_all | solution.py:342
  19.2 6.1 %collective-permute-start.7 = (bf16[1,2,256,128]{3,2,1,0:T(8,128)(2,1)S(1)}, bf16[1,2,256,128]{3,2,1,0:T(8,128)(2,1)S(1)}, u32[]{:S(2)}, u32[]{:S(2)}) collective-permute-start(bf16[1,2,256,128]{3,2,1,0:T(8,128)(2,1)S(1)} %fusion.7.refs_9_), channel_id=1, source_target_pairs={{0,12},{2,14},{4,8},{6,10},{8,4},{10,6},{12,0},{14,2},{1,13},{3,15... | collective-permute-start | bytes 393224 | tf_op jit(solution)/shard_map/ppermute | solution.py:330
  25.3 1.2 collective-permute-start.6
  26.4 1.0 collective-permute-start.5
  27.4 6.4 %attend_1.1 = (f32[1,2,256,128]{3,2,1,0:T(8,128)}, f32[256,2048]{1,0:T(8,128)}) custom-call(s32[1]{0:T(128)} %bitcast.c_ref.refs_0_, bf16[1,128,4096]{2,1,0:T(8,128)(2,1)} %refs_1_.5, bf16[1,128,4096]{2,1,0:T(8,128)(2,1)} %copy-done.7, bf16[1,128,4096]{2,1,0:T(8,128)(2,1)} %refs_3_.5, bf16[1,128,4096]{2,1,0:T(8,128)(2,1)} %copy-done.8, ...), custom_call_target="tpu_custom_call" | custom-call | flops 2684354560 | bytes 8388608 | tf_op jit(solution)/shard_map/attend_1/pallas_call | solution.py:269
  33.8 0.0 collective-permute-done.6
  33.8 4.8 %collective-permute-done.5 = bf16[1,2,256,128]{3,2,1,0:T(8,128)(2,1)S(1)} collective-permute-done((bf16[1,2,256,128]{3,2,1,0:T(8,128)(2,1)S(1)}, bf16[1,2,256,128]{3,2,1,0:T(8,128)(2,1)S(1)}, u32[]{:S(2)}, u32[]{:S(2)}) %collective-permute-start.5) | collective-permute-done | bytes 131104 | tf_op jit(solution)/shard_map/ppermute | solution.py:330
  38.7 1.0 pad_maximum_fusion
  39.6 0.7 collective-permute-start.8
  40.3 0.8 pad_maximum_fusion.1.refs_9_
  41.1 11.8 %attend_3.1 = (f32[3,2,256,128]{3,2,1,0:T(8,128)}, f32[256,2048]{1,0:T(8,128)}) custom-call(s32[1]{0:T(128)} %bitcast.c_ref.refs_0_, bf16[1,128,4096]{2,1,0:T(8,128)(2,1)} %refs_1_.5, bf16[1,128,4096]{2,1,0:T(8,128)(2,1)} %copy-done.7, bf16[1,128,4096]{2,1,0:T(8,128)(2,1)} %refs_3_.5, bf16[1,128,4096]{2,1,0:T(8,128)(2,1)} %copy-done.8, ...), custom_call_target="tpu_custom_call" | custom-call | flops 8053063680 | bytes 8388608 | tf_op jit(solution)/shard_map/attend_3/pallas_call | solution.py:269
  52.9 0.0 collective-permute-done.8.refs_9_
  52.9 0.0 copy-start.10
  52.9 0.8 copy-done.10
  53.7 14.3 %attend_4.1 = (bf16[4,2,256,128]{3,2,1,0:T(8,128)(2,1)}, bf16[1,128,4096]{2,1,0:T(8,128)(2,1)}, bf16[128,2048]{1,0:T(8,128)(2,1)}) custom-call(s32[1]{0:T(128)} %bitcast.c_ref.refs_0_, bf16[1,128,4096]{2,1,0:T(8,128)(2,1)} %refs_1_.5, bf16[1,128,4096]{2,1,0:T(8,128)(2,1)} %copy-done.7, bf16[1,128,4096]{2,1,0:T(8,128)(2,1)} %refs_3_.5, ...), custom_call_target="tpu_custom_call" | custom-call | flops 10737418240 | bytes 8388608 | tf_op jit(solution)/shard_map/attend_4/pallas_call | solution.py:269
  68.0 1.1 collective-permute-start.9
  69.2 2.4 %collective-permute-start.11 = (bf16[4,768,256]{2,1,0:T(8,128)(2,1)}, bf16[4,768,256]{2,1,0:T(8,128)(2,1)}, u32[]{:S(2)}, u32[]{:S(2)}) collective-permute-start(bf16[4,768,256]{2,1,0:T(8,128)(2,1)} %get-tuple-element.54), channel_id=1, source_target_pairs={{0,1},{1,0},{2,3},{3,2},{4,5},{5,4},{6,7},{7,6},{8,9},{9,8},{10,11... | collective-permute-start | bytes 4718600 | tf_op jit(solution)/shard_map/ppermute | solution.py:327
  71.6 8.8 %collective-permute-done.9 = bf16[4,2,256,128]{3,2,1,0:T(8,128)(2,1)S(1)} collective-permute-done((bf16[4,2,256,128]{3,2,1,0:T(8,128)(2,1)}, bf16[4,2,256,128]{3,2,1,0:T(8,128)(2,1)S(1)}, u32[]{:S(2)}, u32[]{:S(2)}) %collective-permute-start.9) | collective-permute-done | bytes 524320 | tf_op jit(solution)/shard_map/ppermute | solution.py:330
  80.3 0.1 convert_element_type.15
  80.4 0.1 fusion
  80.5 2.0 %all-to-all-done.got_ref = bf16[16,128,1024]{2,1,0:T(8,128)(2,1)} async-done(((bf16[16,128,1024]{2,1,0:T(8,128)(2,1)}), bf16[16,128,1024]{2,1,0:T(8,128)(2,1)}, u32[]{:S(2)}, u32[]{:S(2)}) %all-to-all-start) | async-done | bytes 4194336 | tf_op jit(solution)/shard_map/all_to_all | solution.py:342
  82.5 1.3 slice.33
  83.8 0.0 copy-start.3
  83.8 1.3 collective-permute-start.10
  85.1 0.0 collective-permute-done.11.wsib_ref
  85.1 2.3 %collective-permute-done.10.ssib_ref = bf16[16,128,256]{2,1,0:T(8,128)(2,1)S(1)} collective-permute-done((bf16[16,128,256]{2,1,0:T(8,128)(2,1)S(1)}, bf16[16,128,256]{2,1,0:T(8,128)(2,1)S(1)}, u32[]{:S(2)}, u32[]{:S(2)}) %collective-permute-start.10) | collective-permute-done | bytes 1048608 | tf_op jit(solution)/shard_map/ppermute | solution.py:327
  87.4 1.0 copy-done.9
  88.3 7.4 %experts.1 = (f32[4,1,512]{2,1,0:T(1,128)}, bf16[4,1536,256]{2,1,0:T(8,128)(2,1)}, bf16[4,768,256]{2,1,0:T(8,128)(2,1)}) custom-call(s32[1]{0:T(128)} %bitcast.c_ref.refs_0_, bf16[16,128,1024]{2,1,0:T(8,128)(2,1)} %all-to-all-done.got_ref, bf16[16,128,256]{2,1,0:T(8,128)(2,1)} %copy-done.9, bf16[4,1536,256]{2,1,0:T(8,128)(2,1)} %wown_ref.1, ...), custom_call_target="tpu_custom_call" | custom-call | flops 3221225472 | bytes 13631488 | tf_op jit(solution)/shard_map/experts/pallas_call | solution.py:140
  95.7 0.4 collective-permute-start.16
  96.1 0.7 reduce
  96.8 0.1 reshape.77
  96.9 0.1 broadcast_in_dim.19
  97.0 0.7 broadcast_in_dim.20
  97.7 12.2 %all-to-all-start.1 = ((f32[256,1,128]{2,1,0:T(1,128)}), f32[256,1,128]{2,1,0:T(1,128)S(1)}, u32[]{:S(2)}, u32[]{:S(2)}) async-start(f32[256,1,128]{2,1,0:T(1,128)} %bitcast.7), calls=%async_computation.1 | async-start | bytes 262144 | tf_op jit(solution)/shard_map/all_to_all | solution.py:360
  109.9 5.0 %collective-permute-start.14 = (bf16[2,256,128]{2,1,0:T(8,128)(2,1)S(1)}, bf16[2,256,128]{2,1,0:T(8,128)(2,1)S(1)}, u32[]{:S(2)}, u32[]{:S(2)}) collective-permute-start(bf16[2,256,128]{2,1,0:T(8,128)(2,1)S(1)} %get-tuple-element.70), channel_id=1, source_target_pairs={{0,12},{2,14},{4,8},{6,10},{8,4},{10,6},{12,0},{14,2},{1,13},{3,15... | collective-permute-start | bytes 393224 | tf_op jit(solution)/shard_map/ppermute | solution.py:330
  115.0 1.5 %collective-permute-start.13 = (bf16[2,256,128]{2,1,0:T(8,128)(2,1)S(1)}, bf16[2,256,128]{2,1,0:T(8,128)(2,1)S(1)}, u32[]{:S(2)}, u32[]{:S(2)}) collective-permute-start(bf16[2,256,128]{2,1,0:T(8,128)(2,1)S(1)} %get-tuple-element.71), channel_id=1, source_target_pairs={{0,4},{2,6},{4,0},{6,2},{8,12},{10,14},{12,8},{14,10},{1,5},{3,7},... | collective-permute-start | bytes 393224 | tf_op jit(solution)/shard_map/ppermute | solution.py:330
  116.5 0.6 collective-permute-start.12
  117.2 1.5 %collective-permute-start.15 = (bf16[1,128,2048]{2,1,0:T(8,128)(2,1)}, bf16[1,128,2048]{2,1,0:T(8,128)(2,1)S(1)}, u32[]{:S(2)}, u32[]{:S(2)}) collective-permute-start(bf16[1,128,2048]{2,1,0:T(8,128)(2,1)} %bitcast.40), channel_id=1, source_target_pairs={{0,1},{1,0},{2,3},{3,2},{4,5},{5,4},{6,7},{7,6},{8,9},{9,8},{10,11... | collective-permute-start | bytes 1572872 | tf_op jit(solution)/shard_map/ppermute | solution.py:327
  118.7 3.9 %collective-permute-done.14 = bf16[2,256,128]{2,1,0:T(8,128)(2,1)S(1)} collective-permute-done((bf16[2,256,128]{2,1,0:T(8,128)(2,1)S(1)}, bf16[2,256,128]{2,1,0:T(8,128)(2,1)S(1)}, u32[]{:S(2)}, u32[]{:S(2)}) %collective-permute-start.14) | collective-permute-done | bytes 131104 | tf_op jit(solution)/shard_map/ppermute | solution.py:330
  122.5 2.3 %collective-permute-done.13 = bf16[2,256,128]{2,1,0:T(8,128)(2,1)S(1)} collective-permute-done((bf16[2,256,128]{2,1,0:T(8,128)(2,1)S(1)}, bf16[2,256,128]{2,1,0:T(8,128)(2,1)S(1)}, u32[]{:S(2)}, u32[]{:S(2)}) %collective-permute-start.13) | collective-permute-done | bytes 131104 | tf_op jit(solution)/shard_map/ppermute | solution.py:330
  124.8 0.7 copy-done.5
  125.5 2.0 %collective-permute-done.12 = bf16[2,256,128]{2,1,0:T(8,128)(2,1)} collective-permute-done((bf16[2,256,128]{2,1,0:T(8,128)(2,1)S(1)}, bf16[2,256,128]{2,1,0:T(8,128)(2,1)}, u32[]{:S(2)}, u32[]{:S(2)}) %collective-permute-start.12) | collective-permute-done | bytes 131104 | tf_op jit(solution)/shard_map/ppermute | solution.py:330
  127.5 0.0 all-to-all-done.1
  127.5 1.1 fusion.4
  128.7 2.6 %collective-permute-start.17 = (f32[2,128,128]{2,1,0:T(8,128)S(1)}, f32[2,128,128]{2,1,0:T(8,128)S(1)}, u32[]{:S(2)}, u32[]{:S(2)}) collective-permute-start(f32[2,128,128]{2,1,0:T(8,128)S(1)} %get-tuple-element.74), channel_id=1, source_target_pairs={{0,1},{1,0},{2,3},{3,2},{4,5},{5,4},{6,7},{7,6},{8,9},{9,8},{10,11... | collective-permute-start | bytes 393224 | tf_op jit(solution)/shard_map/ppermute | solution.py:327
  131.2 0.9 join_query.1
  132.1 0.1 collective-permute-done.17
  132.2 0.7 maximum_select_fusion
  132.9 1.2 join_down.1
  134.1 2.6 %collect.1 = f32[8,128]{1,0:T(8,128)} custom-call(s32[8,128]{1,0:T(8,128)} %get-tuple-element.68.slot_ref, f32[8,128]{1,0:T(8,128)} %bitcast.37, f32[256,128]{1,0:T(8,128)} %bitcast.31), custom_call_target="tpu_custom_call" | custom-call | flops 8388608 | bytes 262144 | tf_op jit(solution)/shard_map/collect/pallas_call | solution.py:301
  (25 shorter events, 0.1 us)
Async XLA Ops:
  0.6 12.1 %collective-permute-start = (bf16[1,128,4096]{2,1,0:T(8,128)(2,1)}, bf16[1,128,4096]{2,1,0:T(8,128)(2,1)S(1)}, u32[]{:S(2)}, u32[]{:S(2)}) collective-permute-start(bf16[1,128,4096]{2,1,0:T(8,128)(2,1)} %refs_1_.5), channel_id=1, source_target_pairs={{0,1},{1,0},{2,3},{3,2},{4,5},{5,4},{6,7},{7,6},{8,9},{9,8},{10,11... | collective-permute-start | bytes 3145736 | tf_op jit(solution)/shard_map/ppermute | solution.py:327
  4.0 8.8 %collective-permute-start.1 = (bf16[1,128,4096]{2,1,0:T(8,128)(2,1)}, bf16[1,128,4096]{2,1,0:T(8,128)(2,1)S(1)}, u32[]{:S(2)}, u32[]{:S(2)}) collective-permute-start(bf16[1,128,4096]{2,1,0:T(8,128)(2,1)} %refs_3_.5), channel_id=1, source_target_pairs={{0,1},{1,0},{2,3},{3,2},{4,5},{5,4},{6,7},{7,6},{8,9},{9,8},{10,11... | collective-permute-start | bytes 3145736 | tf_op jit(solution)/shard_map/ppermute | solution.py:327
  4.1 8.6 %collective-permute-start.2 = (f32[1,32,128]{2,1,0:T(8,128)}, f32[1,32,128]{2,1,0:T(8,128)S(1)}, u32[]{:S(2)}, u32[]{:S(2)}) collective-permute-start(f32[1,32,128]{2,1,0:T(8,128)} %refs_5_.5), channel_id=1, source_target_pairs={{0,1},{1,0},{2,3},{3,2},{4,5},{5,4},{6,7},{7,6},{8,9},{9,8},{10,11... | collective-permute-start | bytes 49160 | tf_op jit(solution)/shard_map/ppermute | solution.py:327
  4.5 8.2 %collective-permute-start.3 = (f32[1,32,128]{2,1,0:T(8,128)}, f32[1,32,128]{2,1,0:T(8,128)S(1)}, u32[]{:S(2)}, u32[]{:S(2)}) collective-permute-start(f32[1,32,128]{2,1,0:T(8,128)} %refs_7_.5), channel_id=1, source_target_pairs={{0,1},{1,0},{2,3},{3,2},{4,5},{5,4},{6,7},{7,6},{8,9},{9,8},{10,11... | collective-permute-start | bytes 49160 | tf_op jit(solution)/shard_map/ppermute | solution.py:327
  4.6 8.0 %collective-permute-start.4 = (bf16[2,128,256]{2,1,0:T(8,128)(2,1)}, bf16[2,128,256]{2,1,0:T(8,128)(2,1)S(1)}, u32[]{:S(2)}, u32[]{:S(2)}) collective-permute-start(bf16[2,128,256]{2,1,0:T(8,128)(2,1)} %bitcast.34), channel_id=1, source_target_pairs={{0,1},{1,0},{2,3},{3,2},{4,5},{5,4},{6,7},{7,6},{8,9},{9,8},{10,11... | collective-permute-start | bytes 393224 | tf_op jit(solution)/shard_map/ppermute | solution.py:327
  5.0 7.6 %copy-start.6 = (bf16[1,2,128,256]{3,2,1,0:T(8,128)(2,1)S(1)}, bf16[1,2,128,256]{3,2,1,0:T(8,128)(2,1)}, u32[]{:S(2)}) copy-start(bf16[1,2,128,256]{3,2,1,0:T(8,128)(2,1)} %param.14) | copy-start | bytes 393220
  12.7 14.8 %copy-start.2 = (bf16[1,2,256,128]{3,2,1,0:T(8,128)(2,1)}, bf16[1,2,256,128]{3,2,1,0:T(8,128)(2,1)S(1)}, u32[]{:S(2)}) copy-start(bf16[1,2,256,128]{3,2,1,0:T(8,128)(2,1)S(1)} %fusion.7.refs_9_) | copy-start | bytes 393220
  12.7 0.6 copy-start.11
  12.7 0.6 copy-start.12
  12.7 1.0 copy-start.7
  12.7 1.3 copy-start.8
  14.1 68.4 %all-to-all-start = ((bf16[16,128,1024]{2,1,0:T(8,128)(2,1)}), bf16[16,128,1024]{2,1,0:T(8,128)(2,1)}, u32[]{:S(2)}, u32[]{:S(2)}) async-start(bf16[16,128,1024]{2,1,0:T(8,128)(2,1)} %get-tuple-element.38), calls=%async_computation | async-start | bytes 8388608 | tf_op jit(solution)/shard_map/all_to_all | solution.py:342
  19.2 14.7 %collective-permute-start.7 = (bf16[1,2,256,128]{3,2,1,0:T(8,128)(2,1)S(1)}, bf16[1,2,256,128]{3,2,1,0:T(8,128)(2,1)S(1)}, u32[]{:S(2)}, u32[]{:S(2)}) collective-permute-start(bf16[1,2,256,128]{3,2,1,0:T(8,128)(2,1)S(1)} %fusion.7.refs_9_), channel_id=1, source_target_pairs={{0,12},{2,14},{4,8},{6,10},{8,4},{10,6},{12,0},{14,2},{1,13},{3,15... | collective-permute-start | bytes 393224 | tf_op jit(solution)/shard_map/ppermute | solution.py:330
  25.3 8.6 %collective-permute-start.6 = (bf16[1,2,256,128]{3,2,1,0:T(8,128)(2,1)S(1)}, bf16[1,2,256,128]{3,2,1,0:T(8,128)(2,1)S(1)}, u32[]{:S(2)}, u32[]{:S(2)}) collective-permute-start(bf16[1,2,256,128]{3,2,1,0:T(8,128)(2,1)S(1)} %fusion.7.refs_9_), channel_id=1, source_target_pairs={{0,4},{2,6},{4,0},{6,2},{8,12},{10,14},{12,8},{14,10},{1,5},{3,7},... | collective-permute-start | bytes 393224 | tf_op jit(solution)/shard_map/ppermute | solution.py:330
  26.4 12.2 %collective-permute-start.5 = (bf16[1,2,256,128]{3,2,1,0:T(8,128)(2,1)S(1)}, bf16[1,2,256,128]{3,2,1,0:T(8,128)(2,1)S(1)}, u32[]{:S(2)}, u32[]{:S(2)}) collective-permute-start(bf16[1,2,256,128]{3,2,1,0:T(8,128)(2,1)S(1)} %fusion.7.refs_9_), channel_id=1, source_target_pairs={{0,8},{2,10},{4,12},{6,14},{8,0},{10,2},{12,4},{14,6},{1,9},{3,11}... | collective-permute-start | bytes 393224 | tf_op jit(solution)/shard_map/ppermute | solution.py:330
  39.6 13.3 %collective-permute-start.8 = (bf16[4,2,256,128]{3,2,1,0:T(8,128)(2,1)S(1)}, bf16[4,2,256,128]{3,2,1,0:T(8,128)(2,1)S(1)}, u32[]{:S(2)}, u32[]{:S(2)}) collective-permute-start(bf16[4,2,256,128]{3,2,1,0:T(8,128)(2,1)S(1)} %pad_maximum_fusion), channel_id=1, source_target_pairs={{0,2},{2,0},{4,6},{6,4},{8,10},{10,8},{12,14},{14,12},{1,3},{3,1},... | collective-permute-start | bytes 1572872 | tf_op jit(solution)/shard_map/ppermute | solution.py:330
  52.9 0.8 copy-start.10
  53.7 26.7 %copy-start = (f32[3,2,256,128]{3,2,1,0:T(8,128)S(1)}, f32[3,2,256,128]{3,2,1,0:T(8,128)}, u32[]{:S(2)}) copy-start(f32[3,2,256,128]{3,2,1,0:T(8,128)} %get-tuple-element.49) | copy-start | bytes 2359300
  68.0 12.3 %collective-permute-start.9 = (bf16[4,2,256,128]{3,2,1,0:T(8,128)(2,1)}, bf16[4,2,256,128]{3,2,1,0:T(8,128)(2,1)S(1)}, u32[]{:S(2)}, u32[]{:S(2)}) collective-permute-start(bf16[4,2,256,128]{3,2,1,0:T(8,128)(2,1)} %get-tuple-element.51), channel_id=1, source_target_pairs={{0,2},{2,0},{4,6},{6,4},{8,10},{10,8},{12,14},{14,12},{1,3},{3,1},... | collective-permute-start | bytes 1572872 | tf_op jit(solution)/shard_map/ppermute | solution.py:330
  69.2 15.9 %collective-permute-start.11 = (bf16[4,768,256]{2,1,0:T(8,128)(2,1)}, bf16[4,768,256]{2,1,0:T(8,128)(2,1)}, u32[]{:S(2)}, u32[]{:S(2)}) collective-permute-start(bf16[4,768,256]{2,1,0:T(8,128)(2,1)} %get-tuple-element.54), channel_id=1, source_target_pairs={{0,1},{1,0},{2,3},{3,2},{4,5},{5,4},{6,7},{7,6},{8,9},{9,8},{10,11... | collective-permute-start | bytes 4718600 | tf_op jit(solution)/shard_map/ppermute | solution.py:327
  83.8 43.7 %copy-start.3 = (f32[1,2,256,128]{3,2,1,0:T(8,128)S(1)}, f32[1,2,256,128]{3,2,1,0:T(8,128)}, u32[]{:S(2)}) copy-start(f32[1,2,256,128]{3,2,1,0:T(8,128)} %get-tuple-element.63) | copy-start | bytes 786436
  83.8 3.6 %collective-permute-start.10 = (bf16[16,128,256]{2,1,0:T(8,128)(2,1)S(1)}, bf16[16,128,256]{2,1,0:T(8,128)(2,1)S(1)}, u32[]{:S(2)}, u32[]{:S(2)}) collective-permute-start(bf16[16,128,256]{2,1,0:T(8,128)(2,1)S(1)} %slice.33), channel_id=1, source_target_pairs={{0,1},{1,0},{2,3},{3,2},{4,5},{5,4},{6,7},{7,6},{8,9},{9,8},{10,11... | collective-permute-start | bytes 3145736 | tf_op jit(solution)/shard_map/ppermute | solution.py:327
  87.4 1.0 copy-start.9
  95.7 37.2 %collective-permute-start.16 = (bf16[4,768,256]{2,1,0:T(8,128)(2,1)}, bf16[4,768,256]{2,1,0:T(8,128)(2,1)S(1)}, u32[]{:S(2)}, u32[]{:S(2)}) collective-permute-start(bf16[4,768,256]{2,1,0:T(8,128)(2,1)} %get-tuple-element.61), channel_id=1, source_target_pairs={{0,1},{1,0},{2,3},{3,2},{4,5},{5,4},{6,7},{7,6},{8,9},{9,8},{10,11... | collective-permute-start | bytes 4718600 | tf_op jit(solution)/shard_map/ppermute | solution.py:327
  97.7 29.8 %all-to-all-start.1 = ((f32[256,1,128]{2,1,0:T(1,128)}), f32[256,1,128]{2,1,0:T(1,128)S(1)}, u32[]{:S(2)}, u32[]{:S(2)}) async-start(f32[256,1,128]{2,1,0:T(1,128)} %bitcast.7), calls=%async_computation.1 | async-start | bytes 262144 | tf_op jit(solution)/shard_map/all_to_all | solution.py:360
  109.9 12.6 %collective-permute-start.14 = (bf16[2,256,128]{2,1,0:T(8,128)(2,1)S(1)}, bf16[2,256,128]{2,1,0:T(8,128)(2,1)S(1)}, u32[]{:S(2)}, u32[]{:S(2)}) collective-permute-start(bf16[2,256,128]{2,1,0:T(8,128)(2,1)S(1)} %get-tuple-element.70), channel_id=1, source_target_pairs={{0,12},{2,14},{4,8},{6,10},{8,4},{10,6},{12,0},{14,2},{1,13},{3,15... | collective-permute-start | bytes 393224 | tf_op jit(solution)/shard_map/ppermute | solution.py:330
  115.0 9.8 %collective-permute-start.13 = (bf16[2,256,128]{2,1,0:T(8,128)(2,1)S(1)}, bf16[2,256,128]{2,1,0:T(8,128)(2,1)S(1)}, u32[]{:S(2)}, u32[]{:S(2)}) collective-permute-start(bf16[2,256,128]{2,1,0:T(8,128)(2,1)S(1)} %get-tuple-element.71), channel_id=1, source_target_pairs={{0,4},{2,6},{4,0},{6,2},{8,12},{10,14},{12,8},{14,10},{1,5},{3,7},... | collective-permute-start | bytes 393224 | tf_op jit(solution)/shard_map/ppermute | solution.py:330
  116.5 10.9 %collective-permute-start.12 = (bf16[2,256,128]{2,1,0:T(8,128)(2,1)S(1)}, bf16[2,256,128]{2,1,0:T(8,128)(2,1)}, u32[]{:S(2)}, u32[]{:S(2)}) collective-permute-start(bf16[2,256,128]{2,1,0:T(8,128)(2,1)S(1)} %get-tuple-element.72), channel_id=1, source_target_pairs={{0,8},{2,10},{4,12},{6,14},{8,0},{10,2},{12,4},{14,6},{1,9},{3,11}... | collective-permute-start | bytes 393224 | tf_op jit(solution)/shard_map/ppermute | solution.py:330
  117.2 14.1 %collective-permute-start.15 = (bf16[1,128,2048]{2,1,0:T(8,128)(2,1)}, bf16[1,128,2048]{2,1,0:T(8,128)(2,1)S(1)}, u32[]{:S(2)}, u32[]{:S(2)}) collective-permute-start(bf16[1,128,2048]{2,1,0:T(8,128)(2,1)} %bitcast.40), channel_id=1, source_target_pairs={{0,1},{1,0},{2,3},{3,2},{4,5},{5,4},{6,7},{7,6},{8,9},{9,8},{10,11... | collective-permute-start | bytes 1572872 | tf_op jit(solution)/shard_map/ppermute | solution.py:327
  122.5 2.3 %copy-start.4 = (bf16[2,256,128]{2,1,0:T(8,128)(2,1)}, bf16[2,256,128]{2,1,0:T(8,128)(2,1)S(1)}, u32[]{:S(2)}) copy-start(bf16[2,256,128]{2,1,0:T(8,128)(2,1)S(1)} %collective-permute-done.14) | copy-start | bytes 393220
  124.8 0.7 copy-start.5
  127.5 6.7 %copy-start.1 = (f32[256,1,128]{2,1,0:T(1,128)}, f32[256,1,128]{2,1,0:T(1,128)S(1)}, u32[]{:S(2)}) copy-start(f32[256,1,128]{2,1,0:T(1,128)S(1)} %all-to-all-done.1) | copy-start | bytes 393220
  128.7 3.6 %collective-permute-start.17 = (f32[2,128,128]{2,1,0:T(8,128)S(1)}, f32[2,128,128]{2,1,0:T(8,128)S(1)}, u32[]{:S(2)}, u32[]{:S(2)}) collective-permute-start(f32[2,128,128]{2,1,0:T(8,128)S(1)} %get-tuple-element.74), channel_id=1, source_target_pairs={{0,1},{1,0},{2,3},{3,2},{4,5},{5,4},{6,7},{7,6},{8,9},{9,8},{10,11... | collective-permute-start | bytes 393224 | tf_op jit(solution)/shard_map/ppermute | solution.py:327
